TPU v7x, 256 devices: a whole 4x4x8 slice. The times are simulated.
256 devices in a mesh: patch: 128 (over x, z, y), grp: 2 (over core).
Axes of the slice: x: 4, y: 4, z: 8, core: 2. Of those that a mesh axis runs over, the one named last changes fastest.
Arguments:
- right_side: float32 [6, 1024, 128], P(None, ('patch', 'grp')), may hold values from -40 to 40
- patch_blocks: int32 [128], P('patch'), may hold values from 4 to 8, as said below
- send_rows: int32 [128, 2, 4], P('patch'), may hold values from 0 to 7, as said below
- near_cols: int32 [1024, 10], P(('patch', 'grp')), may hold values from 0 to 15, as said below
- near_blocks: float32 [1024, 10, 128, 128], P(('patch', 'grp')), may hold values from -2 to 2
- inverses: float32 [128, 16, 128, 128], P('patch'), may hold values from -1.5 to 1.5
Outputs:
- solution: float32 [6, 1024, 128], P(None, ('patch', 'grp'))
- residual: float32 [6, 1024, 128], P(None, ('patch', 'grp'))
Inputs may be any that keep to these rules, and one draw needn't show every extreme that they name: `patch_blocks`: every patch has 4 to 8 live slots; some patch has all 8 and some has 4. `send_rows`: every sent slot is live in the sending patch. `near_cols`: entry 0 of each row is the row's own slot within its patch.
All inputs are finite; a program needn't handle non-finite values.
Results may differ from a plain program's by a relative error of at most 0.0003.
Values sent between devices are 32-bit elements; how exact they have to be, the bound alone decides.
A program may use at most 64 MiB of HBM per device.

v0:
```python
import jax
import jax.numpy as jnp
from jax import lax
from jax.sharding import PartitionSpec as P

CYCLES = 2


precise = lax.Precision.HIGHEST
epsilon = 1e-06


def from_behind(value, axis, steps):
    count = lax.axis_size(axis)
    pairs = [(source, (source + steps) % count) for source in range(count)]
    return lax.ppermute(value, axis, pairs)


def least_squares(start_norm, lead_dot, lead_norm, upper_dot, lower_dot, tail_norm):
    radius_one = jnp.sqrt(lead_dot * lead_dot + lead_norm * lead_norm)
    cosine_one = lead_dot / radius_one
    sine_one = lead_norm / radius_one
    carried = cosine_one * upper_dot + sine_one * lower_dot
    rotated = cosine_one * lower_dot - sine_one * upper_dot
    radius_two = jnp.sqrt(rotated * rotated + tail_norm * tail_norm)
    coef_two = -start_norm * sine_one * rotated / (radius_two * radius_two)
    coef_one = (start_norm * cosine_one - carried * coef_two) / radius_one
    return (coef_one, coef_two)


def local_dot(first_field, second_field):
    return jnp.sum(first_field * second_field, axis=(1, 2))


def local(right_side, patch_blocks, send_rows, near_cols, near_blocks, inverses):
    member = lax.axis_index("grp")
    slot_count = near_cols.shape[0]
    position = member * slot_count + jnp.arange(slot_count, dtype=jnp.int32)
    live_mask = (position < patch_blocks[0]).astype(jnp.float32)[None, :, None]
    patch_inverse = inverses[0]
    own_inverse = lax.dynamic_slice_in_dim(patch_inverse, member * slot_count, slot_count, 0)

    def extend(vector):
        patch_vector = lax.all_gather(vector, "grp", axis=1, tiled=True)
        received = []
        for column, offset in ((0, 1), (1, -1)):
            picked = jnp.take(patch_vector, send_rows[0, column], axis=1)
            received.append(from_behind(picked, "patch", offset))
        preceding, following = (received[0], received[1])
        return jnp.concatenate([patch_vector, preceding, following], axis=1)

    def near_product(extended):
        gathered = jnp.take(extended, near_cols, axis=1)
        return jnp.einsum("bkij,nbkj->nbi", near_blocks, gathered, precision=precise) * live_mask

    def operate(vector):
        return near_product(extend(vector))

    def precondition(vector):
        extended = extend(vector)
        smoothed = jnp.einsum("eij,nej->nei", patch_inverse, extended, precision=precise)
        defect = vector - near_product(smoothed)
        own_smooth = lax.dynamic_slice_in_dim(smoothed, member * slot_count, slot_count, 1)
        return (
            own_smooth + jnp.einsum("bij,nbj->nbi", own_inverse, defect, precision=precise)
        ) * live_mask

    def orthogonalize(mapped, basis):
        dots_local = jnp.stack([local_dot(mapped, basis_vector) for basis_vector in basis])
        dots = lax.psum(dots_local, ("patch", "grp"))
        for order_index, basis_vector in enumerate(basis):
            mapped = mapped - dots[order_index][:, None, None] * basis_vector
        length = jnp.sqrt(lax.psum(local_dot(mapped, mapped), ("patch", "grp")) + epsilon)
        return (mapped, dots, length)

    source = right_side * live_mask
    solution = jnp.zeros_like(source)
    for restart in range(CYCLES):
        current = source if restart == 0 else source - operate(solution)
        start_norm = jnp.sqrt(lax.psum(local_dot(current, current), ("patch", "grp")) + epsilon)
        basis_first = current / start_norm[:, None, None]
        zeta_one = precondition(basis_first)
        mapped, dots_one, lead_norm = orthogonalize(operate(zeta_one), [basis_first])
        basis_second = mapped / lead_norm[:, None, None]
        zeta_two = precondition(basis_second)
        mapped, dots_two, tail_norm = orthogonalize(operate(zeta_two), [basis_first, basis_second])
        coef_one, coef_two = least_squares(
            start_norm, dots_one[0], lead_norm, dots_two[0], dots_two[1], tail_norm
        )
        solution = (
            solution + coef_one[:, None, None] * zeta_one + coef_two[:, None, None] * zeta_two
        )
    return (solution, source - operate(solution))


def solution(mesh):
    in_specs = (
        P(None, ("patch", "grp"), None),
        P("patch"),
        P("patch", None, None),
        P(("patch", "grp"), None),
        P(("patch", "grp"), None, None, None),
        P("patch", None, None, None),
    )
    out_specs = (P(None, ("patch", "grp"), None), P(None, ("patch", "grp"), None))
    return jax.shard_map(local, mesh=mesh, in_specs=in_specs, out_specs=out_specs, check_vma=False)
```

profile of v0, /device:TPU:1, one launch (start us, length us, event | category | flops | bytes accessed | tf_op | source)
XLA Modules:
  0.0 932.8 jit_solution(14664545333827657215)
XLA Ops:
  2.4 81.4 %psum.70 = f32[6]{0:T(128)S(1)} all-reduce(f32[6]{0:T(128)S(1)} %fusion.108), channel_id=1, replica_groups=mesh['patch'=128,'grp'=2] {'patch','grp'}, use_global_device_ids=true, to_apply=%region_1.0 | all-reduce | flops 6 | bytes 48 | tf_op jit(solution)/shard_map/psum | solution.py:80
  85.3 2.5 all_gather.30
  89.1 6.9 collective-permute-start.1
  97.5 3.0 fusion.32
  101.1 3.0 fusion.25
  105.5 2.4 all_gather.31
  109.2 7.5 collective-permute-start.3
  120.7 77.3 %psum.71 = f32[6]{0:T(128)S(1)} all-reduce(f32[6]{0:T(128)S(1)} %get-tuple-element.26), channel_id=1, replica_groups=mesh['patch'=128,'grp'=2] {'patch','grp'}, use_global_device_ids=true, to_apply=%region_3.6 | all-reduce | flops 6 | bytes 48 | tf_op jit(solution)/shard_map/psum | solution.py:70
  198.2 72.7 %psum.72 = f32[6]{0:T(128)S(1)} all-reduce(f32[6]{0:T(128)S(1)} %multiply_reduce_fusion.9), channel_id=1, replica_groups=mesh['patch'=128,'grp'=2] {'patch','grp'}, use_global_device_ids=true, to_apply=%region_5.8 | all-reduce | flops 6 | bytes 48 | tf_op jit(solution)/shard_map/psum | solution.py:73
  275.1 6.4 collective-permute-start.5
  282.6 3.0 fusion.30
  289.9 3.0 all_gather.33
  294.2 7.2 collective-permute-start.7
  305.5 77.3 %psum.73 = f32[2,6]{1,0:T(2,128)S(1)} all-reduce(f32[2,6]{1,0:T(2,128)S(1)} %pad_maximum_fusion.6), channel_id=1, replica_groups=mesh['patch'=128,'grp'=2] {'patch','grp'}, use_global_device_ids=true, to_apply=%region_8.11 | all-reduce | flops 12 | bytes 96 | tf_op jit(solution)/shard_map/psum | solution.py:70
  383.0 72.7 %psum.74 = f32[6]{0:T(128)S(1)} all-reduce(f32[6]{0:T(128)S(1)} %multiply_reduce_fusion.6), channel_id=1, replica_groups=mesh['patch'=128,'grp'=2] {'patch','grp'}, use_global_device_ids=true, to_apply=%region_10.13 | all-reduce | flops 6 | bytes 48 | tf_op jit(solution)/shard_map/psum | solution.py:73
  459.8 6.5 collective-permute-start.9
  467.9 2.4 multiply_reduce_fusion.5
  470.3 77.5 %psum.75 = f32[6]{0:T(128)S(1)} all-reduce(f32[6]{0:T(128)S(1)} %get-tuple-element.29), channel_id=1, replica_groups=mesh['patch'=128,'grp'=2] {'patch','grp'}, use_global_device_ids=true, to_apply=%region_12.15 | all-reduce | flops 6 | bytes 48 | tf_op jit(solution)/shard_map/psum | solution.py:80
  551.3 6.9 collective-permute-start.11
  559.3 3.0 fusion.28
  566.6 3.0 all_gather.36
  570.9 7.2 collective-permute-start.13
  579.8 2.4 multiply_reduce_fusion.4
  582.2 77.7 %psum.76 = f32[6]{0:T(128)S(1)} all-reduce(f32[6]{0:T(128)S(1)} %get-tuple-element.31), channel_id=1, replica_groups=mesh['patch'=128,'grp'=2] {'patch','grp'}, use_global_device_ids=true, to_apply=%region_14.17 | all-reduce | flops 6 | bytes 48 | tf_op jit(solution)/shard_map/psum | solution.py:70
  660.1 72.7 %psum.77 = f32[6]{0:T(128)S(1)} all-reduce(f32[6]{0:T(128)S(1)} %multiply_reduce_fusion.3), channel_id=1, replica_groups=mesh['patch'=128,'grp'=2] {'patch','grp'}, use_global_device_ids=true, to_apply=%region_16.19 | all-reduce | flops 6 | bytes 48 | tf_op jit(solution)/shard_map/psum | solution.py:73
  736.9 6.4 collective-permute-start.15
  744.3 3.0 fusion.26
  751.6 3.0 all_gather.38
  755.9 7.2 collective-permute-start.17
  767.2 77.3 %psum.78 = f32[2,6]{1,0:T(2,128)S(1)} all-reduce(f32[2,6]{1,0:T(2,128)S(1)} %pad_maximum_fusion.7), channel_id=1, replica_groups=mesh['patch'=128,'grp'=2] {'patch','grp'}, use_global_device_ids=true, to_apply=%region_19.22 | all-reduce | flops 12 | bytes 96 | tf_op jit(solution)/shard_map/psum | solution.py:70
  844.7 72.7 %psum.79 = f32[6]{0:T(128)S(1)} all-reduce(f32[6]{0:T(128)S(1)} %multiply_reduce_fusion), channel_id=1, replica_groups=mesh['patch'=128,'grp'=2] {'patch','grp'}, use_global_device_ids=true, to_apply=%region_21.24 | all-reduce | flops 6 | bytes 48 | tf_op jit(solution)/shard_map/psum | solution.py:73
  921.7 6.4 collective-permute-start.19
  (137 shorter events, 69.6 us)
Async XLA Ops:
  0.6 100.4 %copy-start = (f32[4,10,128,128]{3,2,1,0:T(8,128)S(1)}, f32[4,10,128,128]{3,2,1,0:T(8,128)}, u32[]{:S(2)}) copy-start(f32[4,10,128,128]{3,2,1,0:T(8,128)} %param.14) | copy-start | bytes 7864324
  88.4 9.0 collective-permute-start
  89.1 8.4 collective-permute-start.1
  97.4 20.9 %copy-start.1 = (f32[6,4,128]{2,1,0:T(4,128)S(1)}, f32[6,4,128]{2,1,0:T(4,128)}, u32[]{:S(2)}) copy-start(f32[6,4,128]{2,1,0:T(4,128)} %param.10) | copy-start | bytes 36868
  109.2 8.5 collective-permute-start.2
  109.2 8.5 collective-permute-start.3
  274.4 8.2 collective-permute-start.4
  275.1 7.5 collective-permute-start.5
  294.2 8.3 collective-permute-start.6
  294.2 8.3 collective-permute-start.7
  459.2 8.0 collective-permute-start.8
  459.8 7.5 collective-permute-start.9
  551.3 8.0 collective-permute-start.10
  551.3 8.0 collective-permute-start.11
  570.9 8.3 collective-permute-start.12
  570.9 8.3 collective-permute-start.13
  736.3 8.0 collective-permute-start.14
  736.9 7.5 collective-permute-start.15
  755.9 8.3 collective-permute-start.16
  755.9 8.3 collective-permute-start.17
  920.9 8.2 collective-permute-start.18
  921.7 7.5 collective-permute-start.19
where the time goes:
time: 944 us; the launch traced here: 933 us
  blocking collectives  784 us (83%)
  starting transfers between devices  71.3 us (8%)
  matrix products  41.6 us (4%)
  local copies, waits for them, and re-layouts  18.3 us (2%)
    psum x4, blocking collectives, orthogonalize(): dots = lax.psum(dots_local, ('patch', 'grp'))  310 us
    psum x4, blocking collectives, orthogonalize(): lax.psum(local_dot(mapped, mapped), ('patch', 'grp')) + epsilon  291 us
    psum x2, blocking collectives, local(): lax.psum(local_dot(current, current), ('patch', 'grp')) + epsilon  159 us
    ppermute x20, starting transfers between devices, from_behind(): return lax.ppermute(value, axis, pairs)  71.3 us
    all_gather x10, blocking collectives, extend(): patch_vector = lax.all_gather(vector, 'grp', axis=1, tiled=True)  24.6 us
    dot_general x10, matrix products, near_product(): jnp.einsum('bkij,nbkj->nbi', near_blocks, gathered, precision=precise)  23.9 us
  transfers between devices with their start and end apart: 20, of which 9 were waited for; matrix products, arithmetic and copies ran while one was open for 0% of the time, Pallas kernels for 0%

commit v1 on v0

v1 whole, which is shorter than its diff:
```python
import functools

import jax
import jax.numpy as jnp
from jax import lax
from jax.experimental import pallas as pl
from jax.experimental.pallas import tpu as pltpu
from jax.sharding import PartitionSpec as P

CYCLES = 2
EPSILON = 1e-06
NB = 4
PB = 8
NE = 16
NEAR = 10
BS = 128
NRHS = 6
ROWS = 8
MESH = pl.DeviceIdType.MESH
F32 = jnp.float32
BF16 = jnp.bfloat16


def least_squares(start_norm, lead_dot, lead_norm, upper_dot, lower_dot, tail_norm):
    radius_one = jnp.sqrt(lead_dot * lead_dot + lead_norm * lead_norm)
    cosine_one = lead_dot / radius_one
    sine_one = lead_norm / radius_one
    carried = cosine_one * upper_dot + sine_one * lower_dot
    rotated = cosine_one * lower_dot - sine_one * upper_dot
    radius_two = jnp.sqrt(rotated * rotated + tail_norm * tail_norm)
    coef_two = -start_norm * sine_one * rotated / (radius_two * radius_two)
    coef_one = (start_norm * cosine_one - carried * coef_two) / radius_one
    return (coef_one, coef_two)


def split_three(value):
    high = value.astype(BF16).astype(F32)
    rest = value - high
    middle = rest.astype(BF16).astype(F32)
    return high, middle, rest - middle


def store_parts(ref, index, value):
    high, middle, low = split_three(value)
    ref[index, 0:16, :] = jnp.concatenate([high, middle], axis=0).astype(BF16)
    ref[index, 16:32, :] = jnp.concatenate([low, jnp.zeros_like(low)], axis=0).astype(BF16)


def store_matrix_parts(ref, index, rows, value):
    turned = value.T
    high = turned.astype(BF16)
    ref[index, rows, 0:BS] = high
    ref[index, rows, BS : 2 * BS] = (turned - high.astype(F32)).astype(BF16)


def product(parts, matrix):
    full = lax.dot_general(
        parts, matrix, (((1,), (0,)), ((), ())), preferred_element_type=F32
    )
    high, middle, low = full[0:8], full[8:16], full[16:24]
    smallest = low[:, 0:BS] + middle[:, BS : 2 * BS]
    return high[:, 0:BS] + (middle[:, 0:BS] + high[:, BS : 2 * BS] + smallest)


def kernel(
    shape,
    blocks_ref,
    rows_ref,
    cols_ref,
    right_ref,
    near_ref,
    inverse_ref,
    solution_ref,
    residual_ref,
    right_in,
    near_in,
    inverse_in,
    near_w,
    inverse_w,
    ext_parts,
    smooth_parts,
    smooth,
    defect_parts,
    field,
    picked,
    landed,
    dots,
    landed_dots,
    state,
    load_sem,
    swap_send,
    swap_recv,
    sum_send,
    sum_recv,
):
    size_x, size_z, size_y = shape
    patches = size_x * size_z * size_y
    patch = lax.axis_index("patch")
    core = lax.axis_index("grp")
    place_y = lax.rem(patch, size_y)
    place_z = lax.rem(lax.div(patch, size_y), size_z)
    place_x = lax.div(patch, size_y * size_z)
    before = lax.rem(patch + (patches - 1), patches)
    after = lax.rem(patch + 1, patches)
    other = 1 - core

    counts = (2 * size_z, size_x * size_y)

    def member(phase, offset):
        if phase == 0:
            place = lax.rem(place_z * 2 + core + offset, counts[0])
            spot_z, spot_core = lax.div(place, 2), lax.rem(place, 2)
            return ((place_x * size_z + spot_z) * size_y + place_y, spot_core)
        place = lax.rem(place_x * size_y + place_y + offset, counts[1])
        spot_x, spot_y = lax.div(place, size_y), lax.rem(place, size_y)
        return ((spot_x * size_z + place_z) * size_y + spot_y, core)

    barrier = pltpu.get_barrier_semaphore()
    greeted = 0
    for target in ((patch, other), (before, core), (before, other), (after, core), (after, other)):
        pl.semaphore_signal(barrier, inc=1, device_id=target, device_id_type=MESH)
        greeted += 1
    for phase in range(2):
        for offset in range(1, counts[phase]):
            pl.semaphore_signal(
                barrier, inc=1, device_id=member(phase, offset), device_id_type=MESH
            )
            greeted += 1

    loads = [pltpu.make_async_copy(right_ref, right_in, load_sem.at[0])]
    loads += [pltpu.make_async_copy(inverse_ref.at[0], inverse_in, load_sem.at[1])]
    loads += [
        pltpu.make_async_copy(near_ref.at[b], near_in.at[b], load_sem.at[2 + b])
        for b in range(NB)
    ]
    for load in loads:
        load.start()

    first_slot = core * NB
    live = [
        jnp.where(first_slot + s < blocks_ref[0], jnp.float32(1), jnp.float32(0))
        for s in range(NB)
    ]
    lane = lax.broadcasted_iota(jnp.int32, (ROWS, BS), 1)

    def swap_copies(kind):
        own, to_after, to_before = field.at[kind], picked.at[kind, 0], picked.at[kind, 1]
        plan = (
            (to_after, 1, (after, core)),
            (to_after, 2, (after, other)),
            (to_before, 3, (before, core)),
            (to_before, 4, (before, other)),
            (own, 0, (patch, other)),
        )
        return [
            pltpu.make_async_remote_copy(
                src_ref=source,
                dst_ref=landed.at[kind, slot],
                send_sem=swap_send.at[kind, slot],
                recv_sem=swap_recv.at[kind, slot],
                device_id=target,
                device_id_type=MESH,
            )
            for source, slot, target in plan
        ]

    def start_swap(kind):
        for way in range(2):
            for o in range(NB):
                row = rows_ref[0, way, o]
                mine = jnp.where(
                    jnp.logical_and(row >= first_slot, row < first_slot + NB),
                    jnp.float32(1),
                    jnp.float32(0),
                )
                picked[kind, way, o] = field[kind, jnp.bitwise_and(row, NB - 1)] * mine
        copies = swap_copies(kind)
        for copy in copies:
            copy.start()
        return copies

    def sum_copies(parity, phase):
        return [
            pltpu.make_async_remote_copy(
                src_ref=dots.at[parity, phase],
                dst_ref=landed_dots.at[parity, phase, offset],
                send_sem=sum_send.at[parity, phase, offset],
                recv_sem=sum_recv.at[parity, phase, offset],
                device_id=member(phase, offset),
                device_id_type=MESH,
            )
            for offset in range(1, counts[phase])
        ]

    def start_sum(parity, phase):
        copies = sum_copies(parity, phase)
        for copy in copies:
            copy.start()
        return copies

    def finish_sum(copies, parity, phase):
        total = dots[parity, phase]
        for offset, copy in enumerate(copies, 1):
            copy.wait_recv()
            total = total + landed_dots[parity, phase, offset]
        for copy in copies:
            copy.wait_send()
        return total

    def extend(kind, copies, then):
        for s in range(NB):
            store_parts(ext_parts, first_slot + s, field[kind, s])
            then(first_slot + s)
        copies[4].wait_recv()
        for s in range(NB):
            store_parts(ext_parts, other * NB + s, landed[kind, 0, s])
            then(other * NB + s)
        for way in range(2):
            copies[2 * way].wait_recv()
            copies[1 + 2 * way].wait_recv()
            for o in range(NB):
                value = landed[kind, 1 + 2 * way, o] + landed[kind, 2 + 2 * way, o]
                store_parts(ext_parts, PB + NB * way + o, value)
                then(PB + NB * way + o)

    def near_product(parts_ref, b):
        gathered = jnp.concatenate([parts_ref[cols_ref[b, k]] for k in range(NEAR)], axis=1)
        return product(gathered, near_w[b])

    def smooth_block(e):
        value = product(ext_parts[e], inverse_w[e])
        smooth[e] = value
        store_parts(smooth_parts, e, value)

    def precondition(copies):
        extend(0, copies, smooth_block)
        for b in range(NB):
            defect = field[0, b] - near_product(smooth_parts, b)
            store_parts(defect_parts, b, defect)
        for b in range(NB):
            inner = product(defect_parts[b], inverse_w[first_slot + b])
            field[1, b] = (smooth[first_slot + b] + inner) * live[b]

    def dot_tile(pairs):
        tile = jnp.zeros((ROWS, BS), F32)
        for q, (left, right) in enumerate(pairs):
            partial = left[0] * right[0]
            for s in range(1, NB):
                partial = partial + left[s] * right[s]
            total = jnp.sum(partial, axis=1, keepdims=True)
            tile = jnp.where(lane == q, total, tile)
        return tile

    def pick(tile, q):
        return jnp.broadcast_to(tile[:, q : q + 1], (ROWS, BS))

    loads[0].wait()
    empty = jnp.zeros((ROWS - NRHS, BS), F32)
    for s in range(NB):
        value = jnp.concatenate([right_in[:, s, :], empty], axis=0) * live[s]
        field[0, s] = value
        state[0, s] = value
    source = [state[0, s] for s in range(NB)]
    dots[0, 0] = dot_tile([(source, source)])

    pl.semaphore_wait(barrier, greeted)
    first_copies = start_swap(0)
    loads[1].wait()
    for e in range(NE):
        store_matrix_parts(inverse_w, e, slice(0, BS), inverse_in[e])
    for b in range(NB):
        loads[2 + b].wait()
        for k in range(NEAR):
            store_matrix_parts(near_w, b, slice(k * BS, (k + 1) * BS), near_in[b, k])

    R, FIRST, ZETA1, MAPPED1, SECOND, ZETA2, MAPPED2, RAWZ, RAWM, SOL = range(10)

    def get(index):
        return [state[index, s] for s in range(NB)]

    def put(index, values):
        for s in range(NB):
            state[index, s] = values[s]

    def combine(*terms):
        out = []
        for s in range(NB):
            value = None
            for coefficient, vector in terms:
                term = vector[s] if coefficient is None else coefficient * vector[s]
                value = term if value is None else value + term
            out.append(value)
        return out

    def begin(total):
        square = pick(total, 0)
        norm = jnp.sqrt(square + EPSILON)
        return norm, square / (norm * norm)

    def extend_basis(lead_dot, lead_square, first_square):
        reduced = lead_square - lead_dot * lead_dot * (2.0 - first_square)
        return jnp.sqrt(jnp.maximum(reduced, 0.0) + EPSILON)

    def second_dots(first, second, mapped):
        return dot_tile(
            [(mapped, first), (mapped, second), (mapped, mapped), (first, second), (second, second)]
        )

    def coefficients(total, norm, first_square, lead_dot, lead_norm):
        upper, lower, square, cross, second_square = [pick(total, q) for q in range(5)]
        tail = (
            square
            - upper * upper * (2.0 - first_square)
            - lower * lower * (2.0 - second_square)
            + 2.0 * upper * lower * cross
        )
        tail_norm = jnp.sqrt(jnp.maximum(tail, 0.0) + EPSILON)
        return least_squares(norm, lead_dot, lead_norm, upper, lower, tail_norm)

    zero = jnp.zeros((ROWS, BS), F32)

    def step(i, carry):
        norm, first_square, lead_dot, lead_norm = carry
        parity = lax.rem(i, 2)
        copies = swap_copies(0)
        partial = start_sum(parity, 0)
        precondition(copies)
        for copy in copies:
            copy.wait_send()
        copies = start_swap(1)
        dots[parity, 1] = finish_sum(partial, parity, 0)
        partial = start_sum(parity, 1)
        extend(1, copies, lambda e: None)
        for copy in copies:
            copy.wait_send()
        for b in range(NB):
            field[0, b] = near_product(ext_parts, b) * live[b]
        total = finish_sum(partial, parity, 1)
        return total, norm, first_square, lead_dot, lead_norm

    def zetas():
        return [field[1, s] for s in range(NB)], [field[0, s] for s in range(NB)]

    def advance(i, values):
        for s in range(NB):
            field[0, s] = values[s]
        return start_swap(0)

    def body(i, carry):
        total, norm, first_square, lead_dot, lead_norm = step(i, carry)
        following = 1 - lax.rem(i, 2)
        zeta, mapped = zetas()

        @pl.when(i == 0)
        def _():
            norm_now, _ = begin(total)
            scale = 1.0 / norm_now
            first = combine((scale, get(R)))
            mapped_one = combine((scale, mapped))
            advance(i, mapped_one)
            put(FIRST, first)
            put(ZETA1, combine((scale, zeta)))
            put(MAPPED1, mapped_one)
            dots[following, 0] = dot_tile([(mapped_one, first), (mapped_one, mapped_one)])

        norm_now, square_now = begin(total)
        norm = jnp.where(i == 0, norm_now, norm)
        first_square = jnp.where(i == 0, square_now, first_square)

        lead_now = pick(total, 0)
        lead_norm_now = extend_basis(lead_now, pick(total, 1), first_square)
        lead_dot = jnp.where(i == 1, lead_now, lead_dot)
        lead_norm = jnp.where(i == 1, lead_norm_now, lead_norm)

        @pl.when(i == 1)
        def _():
            scale = 1.0 / lead_norm
            first, zeta_one, mapped_one = get(FIRST), get(ZETA1), get(MAPPED1)
            mapped_two = combine((scale, combine((None, mapped), (-lead_dot, mapped_one))))
            advance(i, mapped_two)
            second = combine((scale, combine((None, mapped_one), (-lead_dot, first))))
            put(RAWZ, zeta)
            put(RAWM, mapped)
            put(ZETA2, combine((scale, combine((None, zeta), (-lead_dot, zeta_one)))))
            put(MAPPED2, mapped_two)
            dots[following, 0] = second_dots(first, second, mapped_two)

        @pl.when(i == 2)
        def _():
            one, two = coefficients(total, norm, first_square, lead_dot, lead_norm)
            mapped_one, mapped_two, zeta_one = get(MAPPED1), get(MAPPED2), get(ZETA1)
            mapped_next = combine((norm, mapped_one), (-one, get(RAWM)), (-two, mapped))
            advance(i, mapped_next)
            current = combine((None, get(R)), (-one, mapped_one), (-two, mapped_two))
            put(SOL, combine((one, zeta_one), (two, get(ZETA2))))
            put(ZETA1, combine((norm, zeta_one), (-one, get(RAWZ)), (-two, zeta)))
            put(MAPPED1, mapped_next)
            put(R, current)
            dots[following, 0] = dot_tile(
                [(current, current), (current, mapped_next), (mapped_next, mapped_next)]
            )

        return total, norm, first_square, lead_dot, lead_norm

    state_now = (zero, zero, zero, zero)
    carry = (zero,) + state_now

    def loop_body(i, carry):
        return body(i, carry[1:])

    carry = lax.fori_loop(0, 3, loop_body, carry)
    total = step(3, carry[1:])[0]
    zeta, mapped = zetas()
    norm, first_square = begin(total)
    inverse_norm = 1.0 / norm
    current = get(R)
    first = combine((inverse_norm, current))
    mapped_one = combine((inverse_norm, get(MAPPED1)))
    zeta_one = combine((inverse_norm, get(ZETA1)))
    lead_dot = pick(total, 1) * inverse_norm * inverse_norm
    lead_norm = extend_basis(
        lead_dot, pick(total, 2) * inverse_norm * inverse_norm, first_square
    )
    scale = 1.0 / lead_norm
    second = combine((scale, combine((None, mapped_one), (-lead_dot, first))))
    mapped_two = combine((scale, combine((inverse_norm, mapped), (-lead_dot, mapped_one))))
    dots[0, 0] = second_dots(first, second, mapped_two)
    partial = start_sum(0, 0)
    zeta_two = combine((scale, combine((inverse_norm, zeta), (-lead_dot, zeta_one))))
    dots[0, 1] = finish_sum(partial, 0, 0)
    total = finish_sum(start_sum(0, 1), 0, 1)
    one, two = coefficients(total, norm, first_square, lead_dot, lead_norm)
    answer = combine((None, get(SOL)), (one, zeta_one), (two, zeta_two))
    left = combine((None, current), (-one, mapped_one), (-two, mapped_two))
    for s in range(NB):
        solution_ref[:, s, :] = answer[s][0:NRHS]
        residual_ref[:, s, :] = left[s][0:NRHS]


def factors(patches):
    known = {128: (4, 8, 4), 8: (2, 2, 2), 4: (1, 2, 2)}
    return known.get(patches, (1, patches, 1))


def local(shape, right_side, patch_blocks, send_rows, near_cols, near_blocks, inverses):
    counts = (2 * shape[1], shape[0] * shape[2])
    most = max(counts)
    field = jax.ShapeDtypeStruct(right_side.shape, F32)
    smem = pl.BlockSpec(memory_space=pltpu.SMEM)
    vmem = pl.BlockSpec(memory_space=pltpu.VMEM)
    anywhere = pl.BlockSpec(memory_space=pl.ANY)
    return pl.pallas_call(
        functools.partial(kernel, shape),
        out_shape=(field, field),
        in_specs=[smem, smem, smem, anywhere, anywhere, anywhere],
        out_specs=(vmem, vmem),
        scratch_shapes=[
            pltpu.VMEM((NRHS, NB, BS), F32),
            pltpu.VMEM((NB, NEAR, BS, BS), F32),
            pltpu.VMEM((NE, BS, BS), F32),
            pltpu.VMEM((NB, NEAR * BS, 2 * BS), BF16),
            pltpu.VMEM((NE, BS, 2 * BS), BF16),
            pltpu.VMEM((NE, 32, BS), BF16),
            pltpu.VMEM((NE, 32, BS), BF16),
            pltpu.VMEM((NE, ROWS, BS), F32),
            pltpu.VMEM((NB, 32, BS), BF16),
            pltpu.VMEM((2, NB, ROWS, BS), F32),
            pltpu.VMEM((2, 2, NB, ROWS, BS), F32),
            pltpu.VMEM((2, 5, NB, ROWS, BS), F32),
            pltpu.VMEM((2, 2, ROWS, BS), F32),
            pltpu.VMEM((2, 2, most, ROWS, BS), F32),
            pltpu.VMEM((10, NB, ROWS, BS), F32),
            pltpu.SemaphoreType.DMA((2 + NB,)),
            pltpu.SemaphoreType.DMA((2, 5)),
            pltpu.SemaphoreType.DMA((2, 5)),
            pltpu.SemaphoreType.DMA((2, 2, most)),
            pltpu.SemaphoreType.DMA((2, 2, most)),
        ],
        compiler_params=pltpu.CompilerParams(
            collective_id=0, has_side_effects=True, vmem_limit_bytes=60 * 1024 * 1024
        ),
        name="gmres",
    )(patch_blocks, send_rows, near_cols, right_side, near_blocks, inverses)


def solution(mesh):
    in_specs = (
        P(None, ("patch", "grp"), None),
        P("patch"),
        P("patch", None, None),
        P(("patch", "grp"), None),
        P(("patch", "grp"), None, None, None),
        P("patch", None, None, None),
    )
    out_specs = (P(None, ("patch", "grp"), None), P(None, ("patch", "grp"), None))
    shape = factors(mesh.shape["patch"])
    return jax.shard_map(
        functools.partial(local, shape),
        mesh=mesh,
        in_specs=in_specs,
        out_specs=out_specs,
        check_vma=False,
    )
```

time: 944 us -> 76.2 us (0.08); the launches traced: 933 us -> 75.8 us
  blocking collectives: 784 us -> 0 us
  Pallas kernels: 0 us -> 71.9 us
  starting transfers between devices: 71.3 us -> 0 us
  matrix products: 41.6 us -> 0 us
  local copies, waits for them, and re-layouts: 18.3 us -> 2.61 us
    psum x10 -> x0, blocking collectives: 759 us -> none  [the longest x4 310 us: orthogonalize(): dots = lax.psum(dots_local, ('patch', 'grp'))]
    pallas_call x0 -> x1, Pallas kernels: none -> 71.9 us  [local(): pl.pallas_call(functools.partial(kernel, shape), out_shape=(field, field)...]
    ppermute x20 -> x0, starting transfers between devices: 71.3 us -> none  [from_behind(): return lax.ppermute(value, axis, pairs)]
    dot_general x18 -> x0, matrix products: 41.6 us -> none  [the longest x10 23.9 us: near_product(): jnp.einsum('bkij,nbkj->nbi', near_blocks, gathered, precision=precise)]
    all_gather x10 -> x0, blocking collectives: 24.6 us -> none  [extend(): patch_vector = lax.all_gather(vector, 'grp', axis=1, tiled=True)]
    gather x30 -> x0, local copies, waits for them, and re-layouts: 17 us -> none  [the longest x20 11 us: extend(): picked = jnp.take(patch_vector, send_rows[0, column], axis=1)]
  transfers between devices with their start and end apart: 20 -> 0, of which waited for: 9 -> 0; matrix products, arithmetic and copies ran while one was open for 0% -> 0% of each run, Pallas kernels for 0% -> 0%
where the time goes in v1:
time: 76.2 us; the launch traced here: 75.8 us
  Pallas kernels  71.9 us (94%)
  local copies, waits for them, and re-layouts  2.61 us (3%)
  between operations  1.28 us (2%)
    pallas_call x1, Pallas kernels, local(): pl.pallas_call(functools.partial(kernel, shape), out_shape=(field, field)...  71.9 us
    unnamed x2, local copies, waits for them, and re-layouts  2.61 us

profile of v1, /device:TPU:1, one launch (start us, length us, event | category | flops | bytes accessed | tf_op | source)
XLA Modules:
  0.0 75.8 jit_solution(900260324804388679)
XLA Ops:
  1.3 71.9 %gmres.1 = (f32[6,4,128]{2,1,0:T(4,128)}, f32[6,4,128]{2,1,0:T(4,128)}) custom-call(s32[1]{0:T(128)S(6)} %copy.10.blocks_ref, s32[1,2,4]{2,1,0:T(2,128)} %rows_ref.1, s32[4,10]{1,0:T(4,128)} %cols_ref.1, f32[6,4,128]{2,1,0:T(4,128)} %right_ref.1, f32[4,10,128,128]{3,2,1,0:T(8,128)} %near_ref.1, f32[1,16,128,128]{3,2,1,0:T(8,128)} %inverse_ref.1), custom_call_target="tpu_custom_call" | custom-call | tf_op jit(solution)/shard_map/gmres/pallas_call | solution.py:452
  73.2 1.3 %copy.11 = f32[6,4,128]{2,1,0:T(4,128)} copy(f32[6,4,128]{2,1,0:T(4,128)} %get-tuple-element.4) | data formatting | bytes 24576
  74.5 1.3 %copy.12 = f32[6,4,128]{2,1,0:T(4,128)} copy(f32[6,4,128]{2,1,0:T(4,128)} %get-tuple-element.5) | data formatting | bytes 24576

commit v2 on v1

--- a/solution.py
+++ b/solution.py
@@ -46,11 +46,15 @@
     ref[index, 16:32, :] = jnp.concatenate([low, jnp.zeros_like(low)], axis=0).astype(BF16)
 
 
-def store_matrix_parts(ref, index, rows, value):
-    turned = value.T
-    high = turned.astype(BF16)
-    ref[index, rows, 0:BS] = high
-    ref[index, rows, BS : 2 * BS] = (turned - high.astype(F32)).astype(BF16)
+def matrix_parts(value, axis):
+    high = value.astype(BF16)
+    return jnp.concatenate([high, (value - high.astype(F32)).astype(BF16)], axis=axis)
+
+
+def matrix_product(left, right):
+    full = jnp.dot(left, right, preferred_element_type=F32)
+    cross = full[0:BS, BS : 2 * BS] + full[BS : 2 * BS, 0:BS] + full[BS : 2 * BS, BS : 2 * BS]
+    return full[0:BS, 0:BS] + cross
 
 
 def product(parts, matrix):
@@ -65,22 +69,21 @@
 def kernel(
     shape,
     blocks_ref,
-    rows_ref,
-    cols_ref,
+    rows_hbm,
+    cols_hbm,
     right_ref,
     near_ref,
     inverse_ref,
-    solution_ref,
-    residual_ref,
+    both_ref,
+    rows_ref,
+    cols_ref,
     right_in,
     near_in,
     inverse_in,
     near_w,
-    inverse_w,
+    mixed_w,
+    inverse_parts,
     ext_parts,
-    smooth_parts,
-    smooth,
-    defect_parts,
     field,
     picked,
     landed,
@@ -133,8 +136,14 @@
         pltpu.make_async_copy(near_ref.at[b], near_in.at[b], load_sem.at[2 + b])
         for b in range(NB)
     ]
-    for load in loads:
+    loads += [
+        pltpu.make_async_copy(source, target, load_sem.at[2 + NB + i])
+        for i, (source, target) in enumerate(((rows_hbm, rows_ref), (cols_hbm, cols_ref)))
+    ]
+    for load in loads[2 + NB :] + loads[: 2 + NB]:
         load.start()
+    for load in loads[2 + NB :]:
+        load.wait()
 
     first_slot = core * NB
     live = [
@@ -142,6 +151,7 @@
         for s in range(NB)
     ]
     lane = lax.broadcasted_iota(jnp.int32, (ROWS, BS), 1)
+    case = lax.broadcasted_iota(jnp.int32, (ROWS, BS), 0)
 
     def swap_copies(kind):
         own, to_after, to_before = field.at[kind], picked.at[kind, 0], picked.at[kind, 1]
@@ -207,39 +217,22 @@
             copy.wait_send()
         return total
 
-    def extend(kind, copies, then):
+    def extend(kind, copies):
         for s in range(NB):
             store_parts(ext_parts, first_slot + s, field[kind, s])
-            then(first_slot + s)
         copies[4].wait_recv()
         for s in range(NB):
             store_parts(ext_parts, other * NB + s, landed[kind, 0, s])
-            then(other * NB + s)
         for way in range(2):
             copies[2 * way].wait_recv()
             copies[1 + 2 * way].wait_recv()
             for o in range(NB):
                 value = landed[kind, 1 + 2 * way, o] + landed[kind, 2 + 2 * way, o]
                 store_parts(ext_parts, PB + NB * way + o, value)
-                then(PB + NB * way + o)
-
-    def near_product(parts_ref, b):
-        gathered = jnp.concatenate([parts_ref[cols_ref[b, k]] for k in range(NEAR)], axis=1)
-        return product(gathered, near_w[b])
-
-    def smooth_block(e):
-        value = product(ext_parts[e], inverse_w[e])
-        smooth[e] = value
-        store_parts(smooth_parts, e, value)
-
-    def precondition(copies):
-        extend(0, copies, smooth_block)
-        for b in range(NB):
-            defect = field[0, b] - near_product(smooth_parts, b)
-            store_parts(defect_parts, b, defect)
-        for b in range(NB):
-            inner = product(defect_parts[b], inverse_w[first_slot + b])
-            field[1, b] = (smooth[first_slot + b] + inner) * live[b]
+
+    def apply_blocks(weights, b):
+        gathered = jnp.concatenate([ext_parts[cols_ref[b, k]] for k in range(NEAR)], axis=1)
+        return product(gathered, weights[b]) * live[b]
 
     def dot_tile(pairs):
         tile = jnp.zeros((ROWS, BS), F32)
@@ -248,11 +241,12 @@
             for s in range(1, NB):
                 partial = partial + left[s] * right[s]
             total = jnp.sum(partial, axis=1, keepdims=True)
-            tile = jnp.where(lane == q, total, tile)
-        return tile
+            tile = jnp.where(lane == q * ROWS + case, total, tile)
+        return jnp.sum(tile, axis=0, keepdims=True)
 
     def pick(tile, q):
-        return jnp.broadcast_to(tile[:, q : q + 1], (ROWS, BS))
+        mine = jnp.where(lane == q * ROWS + case, jnp.broadcast_to(tile, (ROWS, BS)), 0.0)
+        return jnp.broadcast_to(jnp.sum(mine, axis=1, keepdims=True), (ROWS, BS))
 
     loads[0].wait()
     empty = jnp.zeros((ROWS - NRHS, BS), F32)
@@ -267,11 +261,22 @@
     first_copies = start_swap(0)
     loads[1].wait()
     for e in range(NE):
-        store_matrix_parts(inverse_w, e, slice(0, BS), inverse_in[e])
-    for b in range(NB):
-        loads[2 + b].wait()
+        inverse_parts[e] = matrix_parts(inverse_in[e], 1)
+
+    @pl.loop(0, NB)
+    def _(b):
+        pltpu.make_async_copy(near_ref.at[b], near_in.at[b], load_sem.at[2 + b]).wait()
+        own = inverse_in[first_slot + b]
+        own_parts = matrix_parts(own, 0)
         for k in range(NEAR):
-            store_matrix_parts(near_w, b, slice(k * BS, (k + 1) * BS), near_in[b, k])
+            rows = slice(k * BS, (k + 1) * BS)
+            block = near_in[b, k]
+            left = matrix_product(own_parts, matrix_parts(block, 1))
+            value = -matrix_product(matrix_parts(left, 0), inverse_parts[cols_ref[b, k]])
+            if k == 0:
+                value = 2.0 * own + value
+            mixed_w[b, rows, :] = matrix_parts(value.T, 1)
+            near_w[b, rows, :] = matrix_parts(block.T, 1)
 
     R, FIRST, ZETA1, MAPPED1, SECOND, ZETA2, MAPPED2, RAWZ, RAWM, SOL = range(10)
 
@@ -324,17 +329,19 @@
         parity = lax.rem(i, 2)
         copies = swap_copies(0)
         partial = start_sum(parity, 0)
-        precondition(copies)
+        extend(0, copies)
+        for b in range(NB):
+            field[1, b] = apply_blocks(mixed_w, b)
         for copy in copies:
             copy.wait_send()
         copies = start_swap(1)
         dots[parity, 1] = finish_sum(partial, parity, 0)
         partial = start_sum(parity, 1)
-        extend(1, copies, lambda e: None)
+        extend(1, copies)
         for copy in copies:
             copy.wait_send()
         for b in range(NB):
-            field[0, b] = near_product(ext_parts, b) * live[b]
+            field[0, b] = apply_blocks(near_w, b)
         total = finish_sum(partial, parity, 1)
         return total, norm, first_square, lead_dot, lead_norm
 
@@ -403,7 +410,7 @@
         return total, norm, first_square, lead_dot, lead_norm
 
     state_now = (zero, zero, zero, zero)
-    carry = (zero,) + state_now
+    carry = (jnp.zeros((1, BS), F32),) + state_now
 
     def loop_body(i, carry):
         return body(i, carry[1:])
@@ -433,8 +440,8 @@
     answer = combine((None, get(SOL)), (one, zeta_one), (two, zeta_two))
     left = combine((None, current), (-one, mapped_one), (-two, mapped_two))
     for s in range(NB):
-        solution_ref[:, s, :] = answer[s][0:NRHS]
-        residual_ref[:, s, :] = left[s][0:NRHS]
+        both_ref[0, :, s, :] = answer[s][0:NRHS]
+        both_ref[1, :, s, :] = left[s][0:NRHS]
 
 
 def factors(patches):
@@ -445,42 +452,46 @@
 def local(shape, right_side, patch_blocks, send_rows, near_cols, near_blocks, inverses):
     counts = (2 * shape[1], shape[0] * shape[2])
     most = max(counts)
-    field = jax.ShapeDtypeStruct(right_side.shape, F32)
-    smem = pl.BlockSpec(memory_space=pltpu.SMEM)
+    field = jax.ShapeDtypeStruct((2,) + right_side.shape, F32)
     vmem = pl.BlockSpec(memory_space=pltpu.VMEM)
-    anywhere = pl.BlockSpec(memory_space=pl.ANY)
-    return pl.pallas_call(
+    hbm = pl.BlockSpec(memory_space=pltpu.HBM)
+    send_rows, near_cols, right_side, near_blocks, inverses = [
+        pltpu.with_memory_space_constraint(value, pltpu.HBM)
+        for value in (send_rows, near_cols, right_side, near_blocks, inverses)
+    ]
+    both = pl.pallas_call(
         functools.partial(kernel, shape),
-        out_shape=(field, field),
-        in_specs=[smem, smem, smem, anywhere, anywhere, anywhere],
-        out_specs=(vmem, vmem),
+        out_shape=field,
+        in_specs=[pl.BlockSpec(memory_space=pltpu.SMEM)] + [hbm] * 5,
+        out_specs=vmem,
         scratch_shapes=[
+            pltpu.SMEM((1, 2, NB), jnp.int32),
+            pltpu.SMEM((NB, NEAR), jnp.int32),
             pltpu.VMEM((NRHS, NB, BS), F32),
             pltpu.VMEM((NB, NEAR, BS, BS), F32),
             pltpu.VMEM((NE, BS, BS), F32),
             pltpu.VMEM((NB, NEAR * BS, 2 * BS), BF16),
+            pltpu.VMEM((NB, NEAR * BS, 2 * BS), BF16),
             pltpu.VMEM((NE, BS, 2 * BS), BF16),
             pltpu.VMEM((NE, 32, BS), BF16),
-            pltpu.VMEM((NE, 32, BS), BF16),
-            pltpu.VMEM((NE, ROWS, BS), F32),
-            pltpu.VMEM((NB, 32, BS), BF16),
             pltpu.VMEM((2, NB, ROWS, BS), F32),
             pltpu.VMEM((2, 2, NB, ROWS, BS), F32),
             pltpu.VMEM((2, 5, NB, ROWS, BS), F32),
-            pltpu.VMEM((2, 2, ROWS, BS), F32),
-            pltpu.VMEM((2, 2, most, ROWS, BS), F32),
+            pltpu.VMEM((2, 2, 1, BS), F32),
+            pltpu.VMEM((2, 2, most, 1, BS), F32),
             pltpu.VMEM((10, NB, ROWS, BS), F32),
-            pltpu.SemaphoreType.DMA((2 + NB,)),
+            pltpu.SemaphoreType.DMA((4 + NB,)),
             pltpu.SemaphoreType.DMA((2, 5)),
             pltpu.SemaphoreType.DMA((2, 5)),
             pltpu.SemaphoreType.DMA((2, 2, most)),
             pltpu.SemaphoreType.DMA((2, 2, most)),
         ],
         compiler_params=pltpu.CompilerParams(
-            collective_id=0, has_side_effects=True, vmem_limit_bytes=60 * 1024 * 1024
+            collective_id=0, has_side_effects=True, vmem_limit_bytes=32 * 1024 * 1024
         ),
         name="gmres",
     )(patch_blocks, send_rows, near_cols, right_side, near_blocks, inverses)
+    return both[0], both[1]
 
 
 def solution(mesh):

time: 76.2 us -> 70.7 us (0.928)
  Pallas kernels: 71.9 us -> 68.7 us
  local copies, waits for them, and re-layouts: 2.61 us -> 0.61 us
    pallas_call x1, Pallas kernels: 71.9 us -> 68.7 us  [local(): pl.pallas_call(functools.partial(kernel, shape), out_shape=field, in_spec...]
    unnamed x2 -> x0, local copies, waits for them, and re-layouts: 2.61 us -> none
where the time goes in v2:
time: 70.7 us; the launch traced here: 70.6 us
  Pallas kernels  68.7 us (97%)
  between operations  1.28 us (2%)
    pallas_call x1, Pallas kernels, local(): pl.pallas_call(functools.partial(kernel, shape), out_shape=field, in_spec...  68.7 us

profile of v2, /device:TPU:1, one launch (start us, length us, event | category | flops | bytes accessed | tf_op | source)
XLA Modules:
  0.0 70.6 jit_solution(163909037639395794)
XLA Ops:
  1.3 68.7 %gmres.1 = f32[2,6,4,128]{3,2,1,0:T(4,128)S(1)} custom-call(s32[1]{0:T(128)S(6)} %copy.8.blocks_ref, s32[1,2,4]{2,1,0:T(2,128)} %rows_hbm.1, s32[4,10]{1,0:T(4,128)} %cols_hbm.1, f32[6,4,128]{2,1,0:T(4,128)} %right_ref.1, f32[4,10,128,128]{3,2,1,0:T(8,128)} %near_ref.1, f32[1,16,128,128]{3,2,1,0:T(8,128)} %inverse_ref.1), custom_call_target="tpu_custom_call" | custom-call | tf_op jit(solution)/shard_map/gmres/pallas_call | solution.py:462
  70.0 0.6 slice_bitcast_fusion

commit v3 on v2

v3 whole, which is shorter than its diff:
```python
import functools

import jax
import jax.numpy as jnp
from jax import lax
from jax.experimental import pallas as pl
from jax.experimental.pallas import tpu as pltpu
from jax.sharding import PartitionSpec as P

CYCLES = 2
EPSILON = 1e-06
NB = 4
PB = 8
NE = 16
NEAR = 10
BS = 128
NRHS = 6
ROWS = 8
MESH = pl.DeviceIdType.MESH
F32 = jnp.float32
BF16 = jnp.bfloat16


def least_squares(start_norm, lead_dot, lead_norm, upper_dot, lower_dot, tail_norm):
    radius_one = jnp.sqrt(lead_dot * lead_dot + lead_norm * lead_norm)
    cosine_one = lead_dot / radius_one
    sine_one = lead_norm / radius_one
    carried = cosine_one * upper_dot + sine_one * lower_dot
    rotated = cosine_one * lower_dot - sine_one * upper_dot
    radius_two = jnp.sqrt(rotated * rotated + tail_norm * tail_norm)
    coef_two = -start_norm * sine_one * rotated / (radius_two * radius_two)
    coef_one = (start_norm * cosine_one - carried * coef_two) / radius_one
    return (coef_one, coef_two)


def split_three(value):
    high = value.astype(BF16).astype(F32)
    rest = value - high
    middle = rest.astype(BF16).astype(F32)
    return high, middle, rest - middle


def store_parts(ref, index, value):
    high, middle, low = split_three(value)
    ref[index, 0:16, :] = jnp.concatenate([high, middle], axis=0).astype(BF16)
    ref[index, 16:32, :] = jnp.concatenate([low, jnp.zeros_like(low)], axis=0).astype(BF16)


def matrix_parts(value, axis):
    high = value.astype(BF16)
    return jnp.concatenate([high, (value - high.astype(F32)).astype(BF16)], axis=axis)


def matrix_product(left, right):
    full = jnp.dot(left, right, preferred_element_type=F32)
    cross = full[0:BS, BS : 2 * BS] + full[BS : 2 * BS, 0:BS] + full[BS : 2 * BS, BS : 2 * BS]
    return full[0:BS, 0:BS] + cross


def product(parts, matrix):
    full = lax.dot_general(
        parts, matrix, (((1,), (0,)), ((), ())), preferred_element_type=F32
    )
    high, middle, low = full[0:8], full[8:16], full[16:24]
    smallest = low[:, 0:BS] + middle[:, BS : 2 * BS]
    return high[:, 0:BS] + (middle[:, 0:BS] + high[:, BS : 2 * BS] + smallest)


def kernel(
    shape,
    blocks_ref,
    rows_hbm,
    cols_hbm,
    right_ref,
    near_ref,
    inverse_ref,
    both_ref,
    rows_ref,
    cols_ref,
    right_in,
    near_in,
    inverse_in,
    near_w,
    mixed_w,
    inverse_parts,
    ext_parts,
    field,
    picked,
    landed,
    dots,
    landed_dots,
    state,
    scalars,
    early,
    load_sem,
    swap_send,
    swap_recv,
    sum_send,
    sum_recv,
):
    size_x, size_z, size_y = shape
    patches = size_x * size_z * size_y
    patch = lax.axis_index("patch")
    core = lax.axis_index("grp")
    place_y = lax.rem(patch, size_y)
    place_z = lax.rem(lax.div(patch, size_y), size_z)
    place_x = lax.div(patch, size_y * size_z)
    before = lax.rem(patch + (patches - 1), patches)
    after = lax.rem(patch + 1, patches)
    other = 1 - core

    counts = (2 * size_z, size_x * size_y)

    def member(phase, offset):
        if phase == 0:
            place = lax.rem(place_z * 2 + core + offset, counts[0])
            spot_z, spot_core = lax.div(place, 2), lax.rem(place, 2)
            return ((place_x * size_z + spot_z) * size_y + place_y, spot_core)
        place = lax.rem(place_x * size_y + place_y + offset, counts[1])
        spot_x, spot_y = lax.div(place, size_y), lax.rem(place, size_y)
        return ((spot_x * size_z + place_z) * size_y + spot_y, core)

    barrier = pltpu.get_barrier_semaphore()
    greeted = 0
    for target in ((patch, other), (before, core), (before, other), (after, core), (after, other)):
        pl.semaphore_signal(barrier, inc=1, device_id=target, device_id_type=MESH)
        greeted += 1
    loads = [pltpu.make_async_copy(right_ref, right_in, load_sem.at[0])]
    loads += [pltpu.make_async_copy(inverse_ref.at[0], inverse_in, load_sem.at[1])]
    loads += [
        pltpu.make_async_copy(near_ref.at[b], near_in.at[b], load_sem.at[2 + b])
        for b in range(NB)
    ]
    loads += [
        pltpu.make_async_copy(source, target, load_sem.at[2 + NB + i])
        for i, (source, target) in enumerate(((rows_hbm, rows_ref), (cols_hbm, cols_ref)))
    ]
    for load in loads[2 + NB :] + loads[: 2 + NB]:
        load.start()

    for phase in range(2):
        for offset in range(1, counts[phase]):
            pl.semaphore_signal(
                barrier, inc=1, device_id=member(phase, offset), device_id_type=MESH
            )
            greeted += 1

    for load in loads[2 + NB :]:
        load.wait()
    first_slot = core * NB
    live = [
        jnp.where(first_slot + s < blocks_ref[0], jnp.float32(1), jnp.float32(0))
        for s in range(NB)
    ]
    lane = lax.broadcasted_iota(jnp.int32, (ROWS, BS), 1)
    case = lax.broadcasted_iota(jnp.int32, (ROWS, BS), 0)

    def sent_rows(way):
        found = []
        for o in range(NB):
            row = rows_ref[0, way, o]
            inside = jnp.logical_and(row >= first_slot, row < first_slot + NB)
            found.append(
                (jnp.bitwise_and(row, NB - 1), jnp.where(inside, jnp.float32(1), jnp.float32(0)))
            )
        return found

    sent = (sent_rows(0), sent_rows(1))
    far = jnp.where(place_y == 0, 1, 0)
    near = 1 - far

    def swap_copies(kind):
        plan = [(field.at[kind], 4, (patch, other))]
        for way in (near, far):
            neighbour = jnp.where(way == 1, before, after)
            plan = [
                (picked.at[kind, way], 2 * way, (neighbour, core)),
                (picked.at[kind, way], 2 * way + 1, (neighbour, other)),
            ] + plan
        return [
            pltpu.make_async_remote_copy(
                src_ref=source,
                dst_ref=landed.at[kind, slot],
                send_sem=swap_send.at[kind, slot],
                recv_sem=swap_recv.at[kind, slot],
                device_id=target,
                device_id_type=MESH,
            )
            for source, slot, target in plan
        ]

    def start_swap(kind):
        copies = swap_copies(kind)
        for way in range(2):
            for o in range(NB):
                row, mine = sent[way][o]
                picked[kind, way, o] = field[kind, row] * mine
        for copy in copies:
            copy.start()

    def sum_copies(parity, phase):
        return [
            pltpu.make_async_remote_copy(
                src_ref=dots.at[parity, phase],
                dst_ref=landed_dots.at[parity, phase, offset],
                send_sem=sum_send.at[parity, phase, offset],
                recv_sem=sum_recv.at[parity, phase, offset],
                device_id=member(phase, offset),
                device_id_type=MESH,
            )
            for offset in range(1, counts[phase])
        ]

    def finish_sum(parity, phase):
        total = dots[parity, phase]
        for offset, copy in enumerate(sum_copies(parity, phase), 1):
            copy.wait_recv()
            total = total + landed_dots[parity, phase, offset]
        return total

    def end_sends(copies):
        for copy in copies:
            copy.wait_send()

    def landing(kind, slot):
        return pltpu.make_async_remote_copy(
            src_ref=landed.at[kind, slot],
            dst_ref=landed.at[kind, slot],
            send_sem=swap_send.at[kind, slot],
            recv_sem=swap_recv.at[kind, slot],
            device_id=(patch, other),
            device_id_type=MESH,
        )

    def extend_inside(kind):
        for s in range(NB):
            store_parts(ext_parts, first_slot + s, field[kind, s])
        landing(kind, 4).wait_recv()
        for s in range(NB):
            store_parts(ext_parts, other * NB + s, landed[kind, 4, s])

    def extend_outside(kind):
        for way in (far, near):
            landing(kind, 2 * way).wait_recv()
            landing(kind, 2 * way + 1).wait_recv()
            for o in range(NB):
                value = landed[kind, 2 * way, o] + landed[kind, 2 * way + 1, o]
                store_parts(ext_parts, PB + NB * way + o, value)

    def apply_blocks(weights, b):
        gathered = jnp.concatenate([ext_parts[cols_ref[b, k]] for k in range(NEAR)], axis=1)
        return product(gathered, weights[b]) * live[b]

    def dot_lanes(pairs, first=0):
        tile = jnp.zeros((ROWS, BS), F32)
        for q, (left, right) in enumerate(pairs, first):
            partial = left[0] * right[0]
            for s in range(1, NB):
                partial = partial + left[s] * right[s]
            total = jnp.sum(partial, axis=1, keepdims=True)
            tile = jnp.where(lane == q * ROWS + case, total, tile)
        return tile

    def in_row(tile):
        return jnp.sum(tile, axis=0, keepdims=True)

    def pick(tile, q):
        mine = jnp.where(lane == q * ROWS + case, jnp.broadcast_to(tile, (ROWS, BS)), 0.0)
        return jnp.broadcast_to(jnp.sum(mine, axis=1, keepdims=True), (ROWS, BS))

    loads[0].wait()
    empty = jnp.zeros((ROWS - NRHS, BS), F32)
    for s in range(NB):
        value = jnp.concatenate([right_in[:, s, :], empty], axis=0) * live[s]
        field[0, s] = value
        state[0, s] = value
    pl.semaphore_wait(barrier, greeted)
    start_swap(0)
    loads[1].wait()
    for e in range(NE):
        inverse_parts[e] = matrix_parts(inverse_in[e], 1)

    @pl.loop(0, NB)
    def _(b):
        pltpu.make_async_copy(near_ref.at[b], near_in.at[b], load_sem.at[2 + b]).wait()
        own = inverse_in[first_slot + b]
        own_parts = matrix_parts(own, 0)
        for k in range(NEAR):
            rows = slice(k * BS, (k + 1) * BS)
            block = near_in[b, k]
            left = matrix_product(own_parts, matrix_parts(block, 1))
            value = -matrix_product(matrix_parts(left, 0), inverse_parts[cols_ref[b, k]])
            if k == 0:
                value = 2.0 * own + value
            mixed_w[b, rows, :] = matrix_parts(value.T, 1)

    R, RAW1, Z1, FIRST, ZETA1, MAPPED1, SECOND, ZETA2, MAPPED2, RAWZ, RAWM, SOL, PART = range(13)
    NORM, INVERSE, SQUARE, LEAD, LEAD_NORM, FACTOR = range(6)

    def get(index):
        return [state[index, s] for s in range(NB)]

    def put(index, values):
        for s in range(NB):
            state[index, s] = values[s]

    def of_field(kind):
        return [field[kind, s] for s in range(NB)]

    def combine(*terms):
        out = []
        for s in range(NB):
            value = None
            for coefficient, vector in terms:
                term = vector[s] if coefficient is None else coefficient * vector[s]
                value = term if value is None else value + term
            out.append(value)
        return out

    def lead(total):
        square, mixed, mapped_square = [pick(total, q) for q in range(3)]
        norm = jnp.sqrt(square + EPSILON)
        inverse = 1.0 / norm
        first_square = square * inverse * inverse
        lead_dot = mixed * inverse * inverse
        reduced = mapped_square * inverse * inverse - lead_dot * lead_dot * (2.0 - first_square)
        lead_norm = jnp.sqrt(jnp.maximum(reduced, 0.0) + EPSILON)
        scale = 1.0 / lead_norm
        for index, value in (
            (NORM, norm),
            (INVERSE, inverse),
            (SQUARE, first_square),
            (LEAD, lead_dot),
            (LEAD_NORM, lead_norm),
        ):
            scalars[index] = value
        first = combine((inverse, get(R)))
        mapped_one = combine((inverse, get(RAW1)))
        zeta_one = combine((inverse, get(Z1)))
        raw_zeta = combine((inverse, of_field(1)))
        second = combine((scale, combine((None, mapped_one), (-lead_dot, first))))
        put(FIRST, first)
        put(MAPPED1, mapped_one)
        put(ZETA1, zeta_one)
        put(RAWZ, raw_zeta)
        put(SECOND, second)
        put(ZETA2, combine((scale, combine((None, raw_zeta), (-lead_dot, zeta_one)))))
        scalars[FACTOR] = -scale * inverse
        put(PART, combine((-scale * lead_dot, mapped_one)))
        early[...] = dot_lanes([(first, second), (second, second)], 3)

    def coefficients(total):
        upper, lower, square, cross, second_square = [pick(total, q) for q in range(5)]
        tail = (
            square
            - upper * upper * (2.0 - scalars[SQUARE])
            - lower * lower * (2.0 - second_square)
            + 2.0 * upper * lower * cross
        )
        tail_norm = jnp.sqrt(jnp.maximum(tail, 0.0) + EPSILON)
        return least_squares(
            scalars[NORM], scalars[LEAD], scalars[LEAD_NORM], upper, lower, tail_norm
        )

    def restart(total):
        one, two = coefficients(total)
        norm = scalars[NORM]
        mapped_one, zeta_one = get(MAPPED1), get(ZETA1)
        put(SOL, combine((one, zeta_one), (two, get(ZETA2))))
        put(R, combine((None, get(R)), (-one, mapped_one), (-two, get(MAPPED2))))
        put(Z1, combine((norm, zeta_one), (-one, get(RAWZ)), (-two, of_field(1))))
        put(PART, combine((norm, mapped_one), (-one, get(RAWM))))
        scalars[FACTOR] = two

    @pl.loop(0, 2 * CYCLES)
    def _(i):
        parity = lax.rem(i, 2)
        extend_inside(0)

        @pl.when(i >= 1)
        def _():
            dots[parity, 1] = finish_sum(parity, 0)
            copies = sum_copies(parity, 1)
            for copy in copies:
                copy.start()
            end_sends(sum_copies(parity, 0))

        extend_outside(0)
        for b in range(NB):
            field[1, b] = apply_blocks(mixed_w, b)
        start_swap(1)
        end_sends(swap_copies(0))

        @pl.when(i == 0)
        def _():
            for b in range(NB):
                for k in range(NEAR):
                    near_w[b, k * BS : (k + 1) * BS, :] = matrix_parts(near_in[b, k].T, 1)
            put(Z1, of_field(1))

        extend_inside(1)

        @pl.when(parity == 1)
        def _():
            lead(finish_sum(1, 1))
            end_sends(sum_copies(1, 1))

        @pl.when(i == 2)
        def _():
            restart(finish_sum(0, 1))
            end_sends(sum_copies(0, 1))

        extend_outside(1)
        for b in range(NB):
            field[0, b] = apply_blocks(near_w, b)

        @pl.when(i >= 1)
        def _():
            mapped = of_field(0)
            put(RAWM, combine((scalars[INVERSE], mapped)))
            mapped = combine((None, get(PART)), (-scalars[FACTOR], mapped))
            for s in range(NB):
                field[0, s] = mapped[s]

        @pl.when(i < 2 * CYCLES - 1)
        def _():
            start_swap(0)

        @pl.when(parity == 0)
        def _():
            mapped, current = of_field(0), get(R)
            dots[1, 0] = in_row(
                dot_lanes([(current, current), (current, mapped), (mapped, mapped)])
            )
            for copy in sum_copies(1, 0):
                copy.start()
            put(RAW1, mapped)

        @pl.when(parity == 1)
        def _():
            mapped = of_field(0)
            dots[0, 0] = in_row(
                dot_lanes([(mapped, get(FIRST)), (mapped, get(SECOND)), (mapped, mapped)])
                + early[...]
            )
            for copy in sum_copies(0, 0):
                copy.start()
            put(MAPPED2, mapped)

        end_sends(swap_copies(1))

    dots[0, 1] = finish_sum(0, 0)
    for copy in sum_copies(0, 1):
        copy.start()
    end_sends(sum_copies(0, 0))
    one, two = coefficients(finish_sum(0, 1))
    answer = combine((None, get(SOL)), (one, get(ZETA1)), (two, get(ZETA2)))
    left = combine((None, get(R)), (-one, get(MAPPED1)), (-two, get(MAPPED2)))
    for s in range(NB):
        both_ref[0, :, s, :] = answer[s][0:NRHS]
        both_ref[1, :, s, :] = left[s][0:NRHS]
    end_sends(sum_copies(0, 1))


def factors(patches):
    known = {128: (4, 8, 4), 8: (2, 2, 2), 4: (1, 2, 2)}
    return known.get(patches, (1, patches, 1))


def local(shape, right_side, patch_blocks, send_rows, near_cols, near_blocks, inverses):
    counts = (2 * shape[1], shape[0] * shape[2])
    most = max(counts)
    field = jax.ShapeDtypeStruct((2,) + right_side.shape, F32)
    vmem = pl.BlockSpec(memory_space=pltpu.VMEM)
    hbm = pl.BlockSpec(memory_space=pltpu.HBM)
    send_rows, near_cols, right_side, near_blocks, inverses = [
        pltpu.with_memory_space_constraint(value, pltpu.HBM)
        for value in (send_rows, near_cols, right_side, near_blocks, inverses)
    ]
    both = pl.pallas_call(
        functools.partial(kernel, shape),
        out_shape=field,
        in_specs=[pl.BlockSpec(memory_space=pltpu.SMEM)] + [hbm] * 5,
        out_specs=vmem,
        scratch_shapes=[
            pltpu.SMEM((1, 2, NB), jnp.int32),
            pltpu.SMEM((NB, NEAR), jnp.int32),
            pltpu.VMEM((NRHS, NB, BS), F32),
            pltpu.VMEM((NB, NEAR, BS, BS), F32),
            pltpu.VMEM((NE, BS, BS), F32),
            pltpu.VMEM((NB, NEAR * BS, 2 * BS), BF16),
            pltpu.VMEM((NB, NEAR * BS, 2 * BS), BF16),
            pltpu.VMEM((NE, BS, 2 * BS), BF16),
            pltpu.VMEM((NE, 32, BS), BF16),
            pltpu.VMEM((2, NB, ROWS, BS), F32),
            pltpu.VMEM((2, 2, NB, ROWS, BS), F32),
            pltpu.VMEM((2, 5, NB, ROWS, BS), F32),
            pltpu.VMEM((2, 2, 1, BS), F32),
            pltpu.VMEM((2, 2, most, 1, BS), F32),
            pltpu.VMEM((13, NB, ROWS, BS), F32),
            pltpu.VMEM((6, ROWS, BS), F32),
            pltpu.VMEM((ROWS, BS), F32),
            pltpu.SemaphoreType.DMA((4 + NB,)),
            pltpu.SemaphoreType.DMA((2, 5)),
            pltpu.SemaphoreType.DMA((2, 5)),
            pltpu.SemaphoreType.DMA((2, 2, most)),
            pltpu.SemaphoreType.DMA((2, 2, most)),
        ],
        compiler_params=pltpu.CompilerParams(
            collective_id=0, has_side_effects=True, vmem_limit_bytes=32 * 1024 * 1024
        ),
        name="gmres",
    )(patch_blocks, send_rows, near_cols, right_side, near_blocks, inverses)
    return both[0], both[1]


def solution(mesh):
    in_specs = (
        P(None, ("patch", "grp"), None),
        P("patch"),
        P("patch", None, None),
        P(("patch", "grp"), None),
        P(("patch", "grp"), None, None, None),
        P("patch", None, None, None),
    )
    out_specs = (P(None, ("patch", "grp"), None), P(None, ("patch", "grp"), None))
    shape = factors(mesh.shape["patch"])
    return jax.shard_map(
        functools.partial(local, shape),
        mesh=mesh,
        in_specs=in_specs,
        out_specs=out_specs,
        check_vma=False,
    )
```

time: 70.7 us -> 69.5 us (0.983)
  Pallas kernels: 68.7 us -> 67.5 us
    pallas_call x1, Pallas kernels: 68.7 us -> 67.5 us  [local(): pl.pallas_call(functools.partial(kernel, shape), out_shape=field, in_spec...]
where the time goes in v3:
time: 69.5 us; the launch traced here: 69.4 us
  Pallas kernels  67.5 us (97%)
  between operations  1.28 us (2%)
    pallas_call x1, Pallas kernels, local(): pl.pallas_call(functools.partial(kernel, shape), out_shape=field, in_spec...  67.5 us

profile of v3, /device:TPU:1, one launch (start us, length us, event | category | flops | bytes accessed | tf_op | source)
XLA Modules:
  0.0 69.4 jit_solution(2068010304196720135)
XLA Ops:
  1.3 67.5 %gmres.1 = f32[2,6,4,128]{3,2,1,0:T(4,128)S(1)} custom-call(s32[1]{0:T(128)S(6)} %copy.8.blocks_ref, s32[1,2,4]{2,1,0:T(2,128)} %rows_hbm.1, s32[4,10]{1,0:T(4,128)} %cols_hbm.1, f32[6,4,128]{2,1,0:T(4,128)} %right_ref.1, f32[4,10,128,128]{3,2,1,0:T(8,128)} %near_ref.1, f32[1,16,128,128]{3,2,1,0:T(8,128)} %inverse_ref.1), custom_call_target="tpu_custom_call" | custom-call | tf_op jit(solution)/shard_map/gmres/pallas_call | solution.py:480
  68.8 0.6 slice_bitcast_fusion

commit v4 on v3

--- a/solution.py
+++ b/solution.py
@@ -40,15 +40,19 @@
     return high, middle, rest - middle
 
 
-def store_parts(ref, index, value):
+def vector_parts(value):
     high, middle, low = split_three(value)
-    ref[index, 0:16, :] = jnp.concatenate([high, middle], axis=0).astype(BF16)
-    ref[index, 16:32, :] = jnp.concatenate([low, jnp.zeros_like(low)], axis=0).astype(BF16)
-
-
-def matrix_parts(value, axis):
-    high = value.astype(BF16)
-    return jnp.concatenate([high, (value - high.astype(F32)).astype(BF16)], axis=axis)
+    first = jnp.concatenate([high, middle], axis=0).astype(BF16)
+    second = jnp.concatenate([low, jnp.zeros_like(low)], axis=0).astype(BF16)
+    return jnp.concatenate([first, second], axis=0)
+
+
+def matrix_parts(value, axis, count=2):
+    parts = []
+    for _ in range(count):
+        parts.append(value.astype(BF16))
+        value = value - parts[-1].astype(F32)
+    return jnp.concatenate(parts, axis=axis)
 
 
 def matrix_product(left, right):
@@ -57,12 +61,11 @@
     return full[0:BS, 0:BS] + cross
 
 
-def product(parts, matrix):
-    full = lax.dot_general(
-        parts, matrix, (((1,), (0,)), ((), ())), preferred_element_type=F32
-    )
+def gather_parts(full):
     high, middle, low = full[0:8], full[8:16], full[16:24]
     smallest = low[:, 0:BS] + middle[:, BS : 2 * BS]
+    if full.shape[1] == 3 * BS:
+        smallest = smallest + high[:, 2 * BS : 3 * BS]
     return high[:, 0:BS] + (middle[:, 0:BS] + high[:, BS : 2 * BS] + smallest)
 
 
@@ -80,8 +83,10 @@
     right_in,
     near_in,
     inverse_in,
-    near_w,
+    mixed_in,
     mixed_w,
+    near_dense,
+    mixed_dense,
     inverse_parts,
     ext_parts,
     field,
@@ -232,24 +237,63 @@
             device_id_type=MESH,
         )
 
-    def extend_inside(kind):
-        for s in range(NB):
-            store_parts(ext_parts, first_slot + s, field[kind, s])
+    def own_blocks(kind):
+        return [field[kind, s] for s in range(NB)]
+
+    def core_blocks(kind):
         landing(kind, 4).wait_recv()
-        for s in range(NB):
-            store_parts(ext_parts, other * NB + s, landed[kind, 4, s])
-
-    def extend_outside(kind):
-        for way in (far, near):
-            landing(kind, 2 * way).wait_recv()
-            landing(kind, 2 * way + 1).wait_recv()
+        return [landed[kind, 4, s] for s in range(NB)]
+
+    def margin_blocks(kind, way):
+        landing(kind, 2 * way).wait_recv()
+        landing(kind, 2 * way + 1).wait_recv()
+        return [landed[kind, 2 * way, o] + landed[kind, 2 * way + 1, o] for o in range(NB)]
+
+    def apply_first():
+        for base, values in (
+            (first_slot, own_blocks(0)),
+            (other * NB, core_blocks(0)),
+            (PB + NB * far, margin_blocks(0, far)),
+            (PB + NB * near, margin_blocks(0, near)),
+        ):
             for o in range(NB):
-                value = landed[kind, 2 * way, o] + landed[kind, 2 * way + 1, o]
-                store_parts(ext_parts, PB + NB * way + o, value)
-
-    def apply_blocks(weights, b):
-        gathered = jnp.concatenate([ext_parts[cols_ref[b, k]] for k in range(NEAR)], axis=1)
-        return product(gathered, weights[b]) * live[b]
+                ext_parts[base + o] = vector_parts(values[o])
+        for b in range(NB):
+            gathered = jnp.concatenate([ext_parts[cols_ref[b, k]] for k in range(NEAR)], axis=1)
+            full = jnp.dot(gathered, mixed_w[b], preferred_element_type=F32)
+            field[1, b] = gather_parts(full) * live[b]
+
+    def apply_group(weights, base, values):
+        parts = jnp.concatenate([vector_parts(value) for value in values], axis=1)
+        rows = pl.ds(pl.multiple_of(base * BS, NB * BS), NB * BS)
+        full = jnp.dot(parts, weights[rows, :], preferred_element_type=F32)
+        width = full.shape[1] // NB
+        return [gather_parts(full[:, width * b : width * (b + 1)]) for b in range(NB)]
+
+    def apply_dense(kind, weights, meanwhile):
+        total = apply_group(weights, first_slot, own_blocks(kind))
+        part = apply_group(weights, other * NB, core_blocks(kind))
+        total = [total[b] + part[b] for b in range(NB)]
+        part = apply_group(weights, PB + NB * far, margin_blocks(kind, far))
+        total = [total[b] + part[b] for b in range(NB)]
+        meanwhile()
+        part = apply_group(weights, PB + NB * near, margin_blocks(kind, near))
+        for b in range(NB):
+            field[1 - kind, b] = total[b] + part[b]
+
+    def make_dense(weights, blocks, turned):
+        @pl.loop(0, NE)
+        def _(e):
+            rows = pl.ds(pl.multiple_of(e * BS, BS), BS)
+            for b in range(NB):
+                total = jnp.zeros((BS, BS), F32)
+                for k in range(NEAR):
+                    total = total + blocks[b, k] * jnp.where(cols_ref[b, k] == e, live[b], 0.0)
+                if not turned:
+                    total = total.T
+                width = weights.shape[1] // NB
+                columns = slice(width * b, width * (b + 1))
+                weights[rows, columns] = matrix_parts(total, 1, width // BS)
 
     def dot_lanes(pairs, first=0):
         tile = jnp.zeros((ROWS, BS), F32)
@@ -292,7 +336,9 @@
             value = -matrix_product(matrix_parts(left, 0), inverse_parts[cols_ref[b, k]])
             if k == 0:
                 value = 2.0 * own + value
-            mixed_w[b, rows, :] = matrix_parts(value.T, 1)
+            value = value.T
+            mixed_in[b, k] = value
+            mixed_w[b, rows, :] = matrix_parts(value, 1, 3)
 
     R, RAW1, Z1, FIRST, ZETA1, MAPPED1, SECOND, ZETA2, MAPPED2, RAWZ, RAWM, SOL, PART = range(13)
     NORM, INVERSE, SQUARE, LEAD, LEAD_NORM, FACTOR = range(6)
@@ -375,44 +421,41 @@
     @pl.loop(0, 2 * CYCLES)
     def _(i):
         parity = lax.rem(i, 2)
-        extend_inside(0)
-
-        @pl.when(i >= 1)
-        def _():
+
+        def pass_sum():
             dots[parity, 1] = finish_sum(parity, 0)
-            copies = sum_copies(parity, 1)
-            for copy in copies:
+            for copy in sum_copies(parity, 1):
                 copy.start()
             end_sends(sum_copies(parity, 0))
 
-        extend_outside(0)
-        for b in range(NB):
-            field[1, b] = apply_blocks(mixed_w, b)
+        def use_sum():
+            @pl.when(parity == 1)
+            def _():
+                lead(finish_sum(1, 1))
+                end_sends(sum_copies(1, 1))
+
+            @pl.when(i == 2)
+            def _():
+                restart(finish_sum(0, 1))
+                end_sends(sum_copies(0, 1))
+
+        @pl.when(i == 0)
+        def _():
+            apply_first()
+
+        @pl.when(i >= 1)
+        def _():
+            apply_dense(0, mixed_dense, pass_sum)
+
         start_swap(1)
         end_sends(swap_copies(0))
 
         @pl.when(i == 0)
         def _():
-            for b in range(NB):
-                for k in range(NEAR):
-                    near_w[b, k * BS : (k + 1) * BS, :] = matrix_parts(near_in[b, k].T, 1)
+            make_dense(near_dense, near_in, False)
             put(Z1, of_field(1))
 
-        extend_inside(1)
-
-        @pl.when(parity == 1)
-        def _():
-            lead(finish_sum(1, 1))
-            end_sends(sum_copies(1, 1))
-
-        @pl.when(i == 2)
-        def _():
-            restart(finish_sum(0, 1))
-            end_sends(sum_copies(0, 1))
-
-        extend_outside(1)
-        for b in range(NB):
-            field[0, b] = apply_blocks(near_w, b)
+        apply_dense(1, near_dense, use_sum)
 
         @pl.when(i >= 1)
         def _():
@@ -448,6 +491,10 @@
             put(MAPPED2, mapped)
 
         end_sends(swap_copies(1))
+
+        @pl.when(i == 0)
+        def _():
+            make_dense(mixed_dense, mixed_in, True)
 
     dots[0, 1] = finish_sum(0, 0)
     for copy in sum_copies(0, 1):
@@ -488,8 +535,10 @@
             pltpu.VMEM((NRHS, NB, BS), F32),
             pltpu.VMEM((NB, NEAR, BS, BS), F32),
             pltpu.VMEM((NE, BS, BS), F32),
-            pltpu.VMEM((NB, NEAR * BS, 2 * BS), BF16),
-            pltpu.VMEM((NB, NEAR * BS, 2 * BS), BF16),
+            pltpu.VMEM((NB, NEAR, BS, BS), F32),
+            pltpu.VMEM((NB, NEAR * BS, 3 * BS), BF16),
+            pltpu.VMEM((NE * BS, NB * 2 * BS), BF16),
+            pltpu.VMEM((NE * BS, NB * 3 * BS), BF16),
             pltpu.VMEM((NE, BS, 2 * BS), BF16),
             pltpu.VMEM((NE, 32, BS), BF16),
             pltpu.VMEM((2, NB, ROWS, BS), F32),

time: 69.5 us -> 68.2 us (0.981)
  Pallas kernels: 67.5 us -> 66.2 us
    pallas_call x1, Pallas kernels: 67.5 us -> 66.2 us  [local(): pl.pallas_call(functools.partial(kernel, shape), out_shape=field, in_spec...]
where the time goes in v4:
time: 68.2 us; the launch traced here: 68.1 us
  Pallas kernels  66.2 us (97%)
  between operations  1.28 us (2%)
    pallas_call x1, Pallas kernels, local(): pl.pallas_call(functools.partial(kernel, shape), out_shape=field, in_spec...  66.2 us

profile of v4, /device:TPU:1, one launch (start us, length us, event | category | flops | bytes accessed | tf_op | source)
XLA Modules:
  0.0 68.1 jit_solution(8159357800796343897)
XLA Ops:
  1.3 66.2 %gmres.1 = f32[2,6,4,128]{3,2,1,0:T(4,128)S(1)} custom-call(s32[1]{0:T(128)S(6)} %copy.8.blocks_ref, s32[1,2,4]{2,1,0:T(2,128)} %rows_hbm.1, s32[4,10]{1,0:T(4,128)} %cols_hbm.1, f32[6,4,128]{2,1,0:T(4,128)} %right_ref.1, f32[4,10,128,128]{3,2,1,0:T(8,128)} %near_ref.1, f32[1,16,128,128]{3,2,1,0:T(8,128)} %inverse_ref.1), custom_call_target="tpu_custom_call" | custom-call | tf_op jit(solution)/shard_map/gmres/pallas_call | solution.py:527
  67.5 0.6 slice_bitcast_fusion

commit v5 on v4

--- a/solution.py
+++ b/solution.py
@@ -19,18 +19,6 @@
 MESH = pl.DeviceIdType.MESH
 F32 = jnp.float32
 BF16 = jnp.bfloat16
-
-
-def least_squares(start_norm, lead_dot, lead_norm, upper_dot, lower_dot, tail_norm):
-    radius_one = jnp.sqrt(lead_dot * lead_dot + lead_norm * lead_norm)
-    cosine_one = lead_dot / radius_one
-    sine_one = lead_norm / radius_one
-    carried = cosine_one * upper_dot + sine_one * lower_dot
-    rotated = cosine_one * lower_dot - sine_one * upper_dot
-    radius_two = jnp.sqrt(rotated * rotated + tail_norm * tail_norm)
-    coef_two = -start_norm * sine_one * rotated / (radius_two * radius_two)
-    coef_one = (start_norm * cosine_one - carried * coef_two) / radius_one
-    return (coef_one, coef_two)
 
 
 def split_three(value):
@@ -116,6 +104,17 @@
 
     counts = (2 * size_z, size_x * size_y)
 
+    def hops(offset, size):
+        return min(offset, size - offset)
+
+    offsets = (
+        sorted(range(1, counts[0]), key=lambda o: -hops(o, counts[0])),
+        sorted(
+            range(1, counts[1]),
+            key=lambda o: -hops(o // size_y, size_x) - hops(o % size_y, size_y),
+        ),
+    )
+
     def member(phase, offset):
         if phase == 0:
             place = lax.rem(place_z * 2 + core + offset, counts[0])
@@ -144,7 +143,7 @@
         load.start()
 
     for phase in range(2):
-        for offset in range(1, counts[phase]):
+        for offset in offsets[phase]:
             pl.semaphore_signal(
                 barrier, inc=1, device_id=member(phase, offset), device_id_type=MESH
             )
@@ -170,9 +169,9 @@
             )
         return found
 
-    sent = (sent_rows(0), sent_rows(1))
     far = jnp.where(place_y == 0, 1, 0)
     near = 1 - far
+    sent = (sent_rows(far), sent_rows(near))
 
     def swap_copies(kind):
         plan = [(field.at[kind], 4, (patch, other))]
@@ -196,32 +195,45 @@
 
     def start_swap(kind):
         copies = swap_copies(kind)
-        for way in range(2):
+        for turn, way in enumerate((far, near)):
             for o in range(NB):
-                row, mine = sent[way][o]
+                row, mine = sent[turn][o]
                 picked[kind, way, o] = field[kind, row] * mine
-        for copy in copies:
-            copy.start()
+            for copy in copies[2 * turn : 2 * turn + 2]:
+                copy.start()
+        copies[4].start()
 
     def sum_copies(parity, phase):
         return [
             pltpu.make_async_remote_copy(
                 src_ref=dots.at[parity, phase],
                 dst_ref=landed_dots.at[parity, phase, offset],
-                send_sem=sum_send.at[parity, phase, offset],
-                recv_sem=sum_recv.at[parity, phase, offset],
+                send_sem=sum_send.at[parity, phase],
+                recv_sem=sum_recv.at[parity, phase],
                 device_id=member(phase, offset),
                 device_id_type=MESH,
             )
-            for offset in range(1, counts[phase])
+            for offset in offsets[phase]
         ]
 
+    def all_sums(parity, phase):
+        rows = landed_dots.at[parity, phase, pl.ds(1, counts[phase] - 1)]
+        return pltpu.make_async_remote_copy(
+            src_ref=rows,
+            dst_ref=rows,
+            send_sem=sum_send.at[parity, phase],
+            recv_sem=sum_recv.at[parity, phase],
+            device_id=(patch, other),
+            device_id_type=MESH,
+        )
+
     def finish_sum(parity, phase):
-        total = dots[parity, phase]
-        for offset, copy in enumerate(sum_copies(parity, phase), 1):
-            copy.wait_recv()
-            total = total + landed_dots[parity, phase, offset]
-        return total
+        all_sums(parity, phase).wait_recv()
+        rows = [dots[parity, phase]]
+        rows += [landed_dots[parity, phase, offset] for offset in range(1, counts[phase])]
+        while len(rows) > 1:
+            rows = [sum(rows[k : k + 2][1:], rows[k]) for k in range(0, len(rows), 2)]
+        return rows[0]
 
     def end_sends(copies):
         for copy in copies:
@@ -341,7 +353,7 @@
             mixed_w[b, rows, :] = matrix_parts(value, 1, 3)
 
     R, RAW1, Z1, FIRST, ZETA1, MAPPED1, SECOND, ZETA2, MAPPED2, RAWZ, RAWM, SOL, PART = range(13)
-    NORM, INVERSE, SQUARE, LEAD, LEAD_NORM, FACTOR = range(6)
+    NORM, INVERSE, SQUARE, COSINE, SINE, INVERSE_RADIUS, FACTOR = range(7)
 
     def get(index):
         return [state[index, s] for s in range(NB)]
@@ -372,12 +384,14 @@
         reduced = mapped_square * inverse * inverse - lead_dot * lead_dot * (2.0 - first_square)
         lead_norm = jnp.sqrt(jnp.maximum(reduced, 0.0) + EPSILON)
         scale = 1.0 / lead_norm
+        inverse_radius = 1.0 / jnp.sqrt(lead_dot * lead_dot + lead_norm * lead_norm)
         for index, value in (
             (NORM, norm),
             (INVERSE, inverse),
             (SQUARE, first_square),
-            (LEAD, lead_dot),
-            (LEAD_NORM, lead_norm),
+            (COSINE, lead_dot * inverse_radius),
+            (SINE, lead_norm * inverse_radius),
+            (INVERSE_RADIUS, inverse_radius),
         ):
             scalars[index] = value
         first = combine((inverse, get(R)))
@@ -403,10 +417,13 @@
             - lower * lower * (2.0 - second_square)
             + 2.0 * upper * lower * cross
         )
-        tail_norm = jnp.sqrt(jnp.maximum(tail, 0.0) + EPSILON)
-        return least_squares(
-            scalars[NORM], scalars[LEAD], scalars[LEAD_NORM], upper, lower, tail_norm
-        )
+        norm, cosine, sine = scalars[NORM], scalars[COSINE], scalars[SINE]
+        carried = cosine * upper + sine * lower
+        rotated = cosine * lower - sine * upper
+        square_two = rotated * rotated + (jnp.maximum(tail, 0.0) + EPSILON)
+        coef_two = -norm * sine * rotated / square_two
+        coef_one = (norm * cosine - carried * coef_two) * scalars[INVERSE_RADIUS]
+        return coef_one, coef_two
 
     def restart(total):
         one, two = coefficients(total)
@@ -426,18 +443,18 @@
             dots[parity, 1] = finish_sum(parity, 0)
             for copy in sum_copies(parity, 1):
                 copy.start()
-            end_sends(sum_copies(parity, 0))
+            all_sums(parity, 0).wait_send()
 
         def use_sum():
             @pl.when(parity == 1)
             def _():
                 lead(finish_sum(1, 1))
-                end_sends(sum_copies(1, 1))
+                all_sums(1, 1).wait_send()
 
             @pl.when(i == 2)
             def _():
                 restart(finish_sum(0, 1))
-                end_sends(sum_copies(0, 1))
+                all_sums(0, 1).wait_send()
 
         @pl.when(i == 0)
         def _():
@@ -499,14 +516,14 @@
     dots[0, 1] = finish_sum(0, 0)
     for copy in sum_copies(0, 1):
         copy.start()
-    end_sends(sum_copies(0, 0))
+    all_sums(0, 0).wait_send()
     one, two = coefficients(finish_sum(0, 1))
     answer = combine((None, get(SOL)), (one, get(ZETA1)), (two, get(ZETA2)))
     left = combine((None, get(R)), (-one, get(MAPPED1)), (-two, get(MAPPED2)))
     for s in range(NB):
         both_ref[0, :, s, :] = answer[s][0:NRHS]
         both_ref[1, :, s, :] = left[s][0:NRHS]
-    end_sends(sum_copies(0, 1))
+    all_sums(0, 1).wait_send()
 
 
 def factors(patches):
@@ -547,13 +564,13 @@
             pltpu.VMEM((2, 2, 1, BS), F32),
             pltpu.VMEM((2, 2, most, 1, BS), F32),
             pltpu.VMEM((13, NB, ROWS, BS), F32),
-            pltpu.VMEM((6, ROWS, BS), F32),
+            pltpu.VMEM((7, ROWS, BS), F32),
             pltpu.VMEM((ROWS, BS), F32),
             pltpu.SemaphoreType.DMA((4 + NB,)),
             pltpu.SemaphoreType.DMA((2, 5)),
             pltpu.SemaphoreType.DMA((2, 5)),
-            pltpu.SemaphoreType.DMA((2, 2, most)),
-            pltpu.SemaphoreType.DMA((2, 2, most)),
+            pltpu.SemaphoreType.DMA((2, 2)),
+            pltpu.SemaphoreType.DMA((2, 2)),
         ],
         compiler_params=pltpu.CompilerParams(
             collective_id=0, has_side_effects=True, vmem_limit_bytes=32 * 1024 * 1024

time: 68.2 us -> 67 us (0.982)
  Pallas kernels: 66.2 us -> 65 us
    pallas_call x1, Pallas kernels: 66.2 us -> 65 us  [local(): pl.pallas_call(functools.partial(kernel, shape), out_shape=field, in_spec...]
where the time goes in v5:
time: 67 us; the launch traced here: 66.9 us
  Pallas kernels  65 us (97%)
  between operations  1.28 us (2%)
    pallas_call x1, Pallas kernels, local(): pl.pallas_call(functools.partial(kernel, shape), out_shape=field, in_spec...  65 us

profile of v5, /device:TPU:1, one launch (start us, length us, event | category | flops | bytes accessed | tf_op | source)
XLA Modules:
  0.0 66.9 jit_solution(16198343630294619610)
XLA Ops:
  1.3 65.0 %gmres.1 = f32[2,6,4,128]{3,2,1,0:T(4,128)S(1)} custom-call(s32[1]{0:T(128)S(6)} %copy.8.blocks_ref, s32[1,2,4]{2,1,0:T(2,128)} %rows_hbm.1, s32[4,10]{1,0:T(4,128)} %cols_hbm.1, f32[6,4,128]{2,1,0:T(4,128)} %right_ref.1, f32[4,10,128,128]{3,2,1,0:T(8,128)} %near_ref.1, f32[1,16,128,128]{3,2,1,0:T(8,128)} %inverse_ref.1), custom_call_target="tpu_custom_call" | custom-call | tf_op jit(solution)/shard_map/gmres/pallas_call | solution.py:544
  66.3 0.6 slice_bitcast_fusion

commit v6 on v5

--- a/solution.py
+++ b/solution.py
@@ -124,6 +124,7 @@
         spot_x, spot_y = lax.div(place, size_y), lax.rem(place, size_y)
         return ((spot_x * size_z + place_z) * size_y + spot_y, core)
 
+    landed[...] = jnp.zeros_like(landed)
     barrier = pltpu.get_barrier_semaphore()
     greeted = 0
     for target in ((patch, other), (before, core), (before, other), (after, core), (after, other)):
@@ -174,17 +175,18 @@
     sent = (sent_rows(far), sent_rows(near))
 
     def swap_copies(kind):
-        plan = [(field.at[kind], 4, (patch, other))]
+        cases = pl.ds(0, NRHS)
+        plan = [(field.at[kind, :, cases], 4, (patch, other))]
         for way in (near, far):
             neighbour = jnp.where(way == 1, before, after)
             plan = [
-                (picked.at[kind, way], 2 * way, (neighbour, core)),
-                (picked.at[kind, way], 2 * way + 1, (neighbour, other)),
+                (picked.at[kind, way, :, cases], 2 * way, (neighbour, core)),
+                (picked.at[kind, way, :, cases], 2 * way + 1, (neighbour, other)),
             ] + plan
         return [
             pltpu.make_async_remote_copy(
                 src_ref=source,
-                dst_ref=landed.at[kind, slot],
+                dst_ref=landed.at[kind, slot, :, cases],
                 send_sem=swap_send.at[kind, slot],
                 recv_sem=swap_recv.at[kind, slot],
                 device_id=target,
@@ -240,9 +242,10 @@
             copy.wait_send()
 
     def landing(kind, slot):
+        blocks = landed.at[kind, slot, :, pl.ds(0, NRHS)]
         return pltpu.make_async_remote_copy(
-            src_ref=landed.at[kind, slot],
-            dst_ref=landed.at[kind, slot],
+            src_ref=blocks,
+            dst_ref=blocks,
             send_sem=swap_send.at[kind, slot],
             recv_sem=swap_recv.at[kind, slot],
             device_id=(patch, other),

time: 67 us -> 66.7 us (level)
  no operation moved by 1% of the time
where the time goes in v6:
time: 66.7 us; the launch traced here: 66.6 us
  Pallas kernels  64.7 us (97%)
  between operations  1.28 us (2%)
    pallas_call x1, Pallas kernels, local(): pl.pallas_call(functools.partial(kernel, shape), out_shape=field, in_spec...  64.7 us

profile of v6, /device:TPU:1, one launch (start us, length us, event | category | flops | bytes accessed | tf_op | source)
XLA Modules:
  0.0 66.6 jit_solution(15400974110002040306)
XLA Ops:
  1.3 64.7 %gmres.1 = f32[2,6,4,128]{3,2,1,0:T(4,128)S(1)} custom-call(s32[1]{0:T(128)S(6)} %copy.8.blocks_ref, s32[1,2,4]{2,1,0:T(2,128)} %rows_hbm.1, s32[4,10]{1,0:T(4,128)} %cols_hbm.1, f32[6,4,128]{2,1,0:T(4,128)} %right_ref.1, f32[4,10,128,128]{3,2,1,0:T(8,128)} %near_ref.1, f32[1,16,128,128]{3,2,1,0:T(8,128)} %inverse_ref.1), custom_call_target="tpu_custom_call" | custom-call | tf_op jit(solution)/shard_map/gmres/pallas_call | solution.py:547
  66.0 0.6 slice_bitcast_fusion

commit v7 on v5

--- a/solution.py
+++ b/solution.py
@@ -125,10 +125,6 @@
         return ((spot_x * size_z + place_z) * size_y + spot_y, core)
 
     barrier = pltpu.get_barrier_semaphore()
-    greeted = 0
-    for target in ((patch, other), (before, core), (before, other), (after, core), (after, other)):
-        pl.semaphore_signal(barrier, inc=1, device_id=target, device_id_type=MESH)
-        greeted += 1
     loads = [pltpu.make_async_copy(right_ref, right_in, load_sem.at[0])]
     loads += [pltpu.make_async_copy(inverse_ref.at[0], inverse_in, load_sem.at[1])]
     loads += [
@@ -139,7 +135,13 @@
         pltpu.make_async_copy(source, target, load_sem.at[2 + NB + i])
         for i, (source, target) in enumerate(((rows_hbm, rows_ref), (cols_hbm, cols_ref)))
     ]
-    for load in loads[2 + NB :] + loads[: 2 + NB]:
+    for load in loads[2 + NB :] + loads[:1]:
+        load.start()
+    greeted = 0
+    for target in ((patch, other), (before, core), (before, other), (after, core), (after, other)):
+        pl.semaphore_signal(barrier, inc=1, device_id=target, device_id_type=MESH)
+        greeted += 1
+    for load in loads[1 : 2 + NB]:
         load.start()
 
     for phase in range(2):
@@ -282,7 +284,7 @@
         width = full.shape[1] // NB
         return [gather_parts(full[:, width * b : width * (b + 1)]) for b in range(NB)]
 
-    def apply_dense(kind, weights, meanwhile):
+    def apply_dense(kind, weights, meanwhile, finish):
         total = apply_group(weights, first_slot, own_blocks(kind))
         part = apply_group(weights, other * NB, core_blocks(kind))
         total = [total[b] + part[b] for b in range(NB)]
@@ -291,7 +293,7 @@
         meanwhile()
         part = apply_group(weights, PB + NB * near, margin_blocks(kind, near))
         for b in range(NB):
-            field[1 - kind, b] = total[b] + part[b]
+            field[1 - kind, b] = finish(b, total[b] + part[b])
 
     def make_dense(weights, blocks, turned):
         @pl.loop(0, NE)
@@ -435,6 +437,10 @@
         put(PART, combine((norm, mapped_one), (-one, get(RAWM))))
         scalars[FACTOR] = two
 
+    state[PART] = jnp.zeros((NB, ROWS, BS), F32)
+    scalars[INVERSE] = jnp.zeros((ROWS, BS), F32)
+    scalars[FACTOR] = jnp.full((ROWS, BS), -1.0, F32)
+
     @pl.loop(0, 2 * CYCLES)
     def _(i):
         parity = lax.rem(i, 2)
@@ -462,7 +468,7 @@
 
         @pl.when(i >= 1)
         def _():
-            apply_dense(0, mixed_dense, pass_sum)
+            apply_dense(0, mixed_dense, pass_sum, lambda b, value: value)
 
         start_swap(1)
         end_sends(swap_copies(0))
@@ -472,15 +478,11 @@
             make_dense(near_dense, near_in, False)
             put(Z1, of_field(1))
 
-        apply_dense(1, near_dense, use_sum)
-
-        @pl.when(i >= 1)
-        def _():
-            mapped = of_field(0)
-            put(RAWM, combine((scalars[INVERSE], mapped)))
-            mapped = combine((None, get(PART)), (-scalars[FACTOR], mapped))
-            for s in range(NB):
-                field[0, s] = mapped[s]
+        def to_next(b, value):
+            state[RAWM, b] = scalars[INVERSE] * value
+            return state[PART, b] - scalars[FACTOR] * value
+
+        apply_dense(1, near_dense, use_sum, to_next)
 
         @pl.when(i < 2 * CYCLES - 1)
         def _():

time: 67 us -> 67 us (level)
  no operation moved by 1% of the time
where the time goes in v7:
time: 67 us; the launch traced here: 66.9 us
  Pallas kernels  65 us (97%)
  between operations  1.28 us (2%)
    pallas_call x1, Pallas kernels, local(): pl.pallas_call(functools.partial(kernel, shape), out_shape=field, in_spec...  65 us

profile of v7, /device:TPU:1, one launch (start us, length us, event | category | flops | bytes accessed | tf_op | source)
XLA Modules:
  0.0 66.9 jit_solution(10638634089546604553)
XLA Ops:
  1.3 65.0 %gmres.1 = f32[2,6,4,128]{3,2,1,0:T(4,128)S(1)} custom-call(s32[1]{0:T(128)S(6)} %copy.8.blocks_ref, s32[1,2,4]{2,1,0:T(2,128)} %rows_hbm.1, s32[4,10]{1,0:T(4,128)} %cols_hbm.1, f32[6,4,128]{2,1,0:T(4,128)} %right_ref.1, f32[4,10,128,128]{3,2,1,0:T(8,128)} %near_ref.1, f32[1,16,128,128]{3,2,1,0:T(8,128)} %inverse_ref.1), custom_call_target="tpu_custom_call" | custom-call | tf_op jit(solution)/shard_map/gmres/pallas_call | solution.py:546
  66.3 0.6 slice_bitcast_fusion

commit v8 on v6

--- a/solution.py
+++ b/solution.py
@@ -465,9 +465,14 @@
 
         @pl.when(i >= 1)
         def _():
-            apply_dense(0, mixed_dense, pass_sum)
+            apply_dense(0, mixed_dense, lambda: None)
 
         start_swap(1)
+
+        @pl.when(i >= 1)
+        def _():
+            pass_sum()
+
         end_sends(swap_copies(0))
 
         @pl.when(i == 0)

time: 66.7 us -> 66.6 us (level)
  no operation moved by 1% of the time
where the time goes in v8:
time: 66.6 us; the launch traced here: 66.5 us
  Pallas kernels  64.6 us (97%)
  between operations  1.28 us (2%)
    pallas_call x1, Pallas kernels, local(): pl.pallas_call(functools.partial(kernel, shape), out_shape=field, in_spec...  64.6 us

profile of v8, /device:TPU:1, one launch (start us, length us, event | category | flops | bytes accessed | tf_op | source)
XLA Modules:
  0.0 66.5 jit_solution(2773272474367087683)
XLA Ops:
  1.3 64.6 %gmres.1 = f32[2,6,4,128]{3,2,1,0:T(4,128)S(1)} custom-call(s32[1]{0:T(128)S(6)} %copy.8.blocks_ref, s32[1,2,4]{2,1,0:T(2,128)} %rows_hbm.1, s32[4,10]{1,0:T(4,128)} %cols_hbm.1, f32[6,4,128]{2,1,0:T(4,128)} %right_ref.1, f32[4,10,128,128]{3,2,1,0:T(8,128)} %near_ref.1, f32[1,16,128,128]{3,2,1,0:T(8,128)} %inverse_ref.1), custom_call_target="tpu_custom_call" | custom-call | tf_op jit(solution)/shard_map/gmres/pallas_call | solution.py:552
  65.9 0.6 slice_bitcast_fusion
